TPU v7x, 32 devices: a whole 2x2x4 slice. The times are simulated.
32 devices in a mesh: gx: 2 (over y), gy: 16 (over z, x, core).
Axes of the slice: x: 2, y: 2, z: 4, core: 2. Of those that a mesh axis runs over, the one named last changes fastest.
Arguments:
- source: float32 [64, 4096], P('gx', 'gy'), may hold values from -6 to 6
- potential: float32 [64, 4096], P('gx', 'gy'), may hold values from -1.5 to 1.5
- mobility_along: float32 [64, 4096], P('gx', 'gy'), may hold values from 0.3 to 3
- mobility_across: float32 [64, 4096], P('gx', 'gy'), may hold values from 0.3 to 3
- recombination: float32 [64, 4096], P('gx', 'gy'), may hold values from 0.002 to 0.05
- counts: int32 [2, 16], P('gx', 'gy'), may hold values from 8 to 32, as said below
- basis: float32 [64, 294912], P('gx', 'gy'), may hold values from -1 to 1
- coarse_inverse: float32 [1024, 1024], P(('gx', 'gy')), may hold values from -8 to 8
Outputs:
- solution: float32 [64, 4096], P('gx', 'gy')
- residual: float32 [64, 4096], P('gx', 'gy')
Inputs may be any that keep to these rules, and one draw needn't show every extreme that they name: `counts`: the number of a subdomain's rows of basis that are in use.
All inputs are finite; a program needn't handle non-finite values.
Results may differ from a plain program's by a relative error of at most 0.003.
Values sent between devices are 32-bit elements; how exact they have to be, the bound alone decides.
A program may use at most 64 MiB of HBM per device.

v0:
```python
import jax
import jax.numpy as jnp
from jax import lax
from jax.sharding import PartitionSpec as P

OV = 16
SWEEPS = 8


OMEGA = 0.8
EPSILON = 1e-06
HIGHEST_PRECISION = lax.Precision.HIGHEST


def padded(cells, sides, width):
    for axis, dim in sides:
        count = lax.axis_size(axis)
        ends = count - 1
        head = lax.slice_in_dim(cells, 0, width, axis=dim)
        tail = lax.slice_in_dim(cells, cells.shape[dim] - width, cells.shape[dim], axis=dim)
        cells = jnp.concatenate(
            [
                lax.ppermute(tail, axis, [(i, (i + 1) % count) for i in range(ends)]),
                cells,
                lax.ppermute(head, axis, [((i + 1) % count, i) for i in range(ends)]),
            ],
            axis=dim,
        )
    return cells


def face_weights(potential, mobility_along, mobility_across):
    along_first = jnp.sqrt(mobility_along[:-1, :] * mobility_along[1:, :])
    along_second = jnp.sqrt(mobility_across[:, :-1] * mobility_across[:, 1:])
    rise_first = potential[1:, :] - potential[:-1, :]
    rise_second = potential[:, 1:] - potential[:, :-1]
    downward = along_first * jnp.exp(0.5 * rise_first)
    upward = along_first * jnp.exp(-0.5 * rise_first)
    eastward = along_second * jnp.exp(0.5 * rise_second)
    westward = along_second * jnp.exp(-0.5 * rise_second)
    return (downward, upward, eastward, westward)


def build(potential, mobility_along, mobility_across, recombination):
    downward, upward, eastward, westward = face_weights(potential, mobility_along, mobility_across)
    diagonal = (
        recombination + jnp.pad(upward, ((0, 1), (0, 0))) + jnp.pad(downward, ((1, 0), (0, 0)))
    )
    diagonal = diagonal + jnp.pad(westward, ((0, 0), (0, 1))) + jnp.pad(eastward, ((0, 0), (1, 0)))
    return (diagonal, (downward, upward, eastward, westward))


def coupled(field, faces):
    downward, upward, eastward, westward = faces
    total = jnp.pad(downward * field[1:, :], ((0, 1), (0, 0)))
    total = total + jnp.pad(upward * field[:-1, :], ((1, 0), (0, 0)))
    total = total + jnp.pad(eastward * field[:, 1:], ((0, 0), (0, 1)))
    total = total + jnp.pad(westward * field[:, :-1], ((0, 0), (1, 0)))
    return total


def smooth(vector_patch, diagonal, faces):
    field = jnp.zeros_like(vector_patch)
    for sweep in range(SWEEPS):
        field = (
            field + OMEGA * (vector_patch - (diagonal * field - coupled(field, faces))) / diagonal
        )
    return field


def least_squares(
    source_norm, first_first, second_first, first_second, second_second, third_second
):
    radius = jnp.sqrt(first_first * first_first + second_first * second_first)
    cosine = first_first / radius
    sine = second_first / radius
    upper_right = cosine * first_second + sine * second_second
    lower_right = cosine * second_second - sine * first_second
    radius_two = jnp.sqrt(lower_right * lower_right + third_second * third_second)
    weight_two = lower_right / radius_two * (-sine * source_norm) / radius_two
    weight_one = (cosine * source_norm - upper_right * weight_two) / radius
    remainder_one = source_norm - first_first * weight_one - first_second * weight_two
    remainder_two = -second_first * weight_one - second_second * weight_two
    remainder_three = -third_second * weight_two
    return (weight_one, weight_two, remainder_one, remainder_two, remainder_three)


def extend(stacked):
    return padded(stacked, (("gx", 1), ("gy", 2)), OV)


def totals(values):
    return lax.psum(values, ("gx", "gy"))


def fold(part):
    edges = jnp.concatenate([part[:OV], part[-OV:]], axis=0)
    arrived = padded(edges, (("gx", 0),), OV)
    middle = part[OV:-OV]
    middle = middle.at[:OV].add(arrived[:OV])
    middle = middle.at[-OV:].add(arrived[-OV:])
    sides = jnp.concatenate([middle[:, :OV], middle[:, -OV:]], axis=1)
    arrived = padded(sides, (("gy", 1),), OV)
    inner = middle[:, OV:-OV]
    inner = inner.at[:, :OV].add(arrived[:, :OV])
    inner = inner.at[:, -OV:].add(arrived[:, -OV:])
    return inner


def on_device(
    source, potential, mobility_along, mobility_across, recombination, counts, basis, coarse_inverse
):
    height, breadth = source.shape
    vectors = basis.shape[0]
    grown = extend(jnp.stack([source, potential, mobility_along, mobility_across, recombination]))
    source_patch = grown[0]
    diagonal, faces = build(grown[1], grown[2], grown[3], grown[4])
    row_place = (
        lax.axis_index("gx") * height - OV + lax.broadcasted_iota(jnp.int32, source_patch.shape, 0)
    )
    column_place = (
        lax.axis_index("gy") * breadth - OV + lax.broadcasted_iota(jnp.int32, source_patch.shape, 1)
    )
    inside = (
        (row_place >= 0)
        & (row_place < height * lax.axis_size("gx"))
        & (column_place >= 0)
        & (column_place < breadth * lax.axis_size("gy"))
    ).astype(jnp.float32)
    smooth_diagonal = diagonal + (1.0 - inside)
    window = grown[1:, OV - 1 : OV + height + 1, OV - 1 : OV + breadth + 1]
    window_diagonal, window_faces = build(window[0], window[1], window[2], window[3])
    count = counts[0, 0]
    live = (lax.broadcasted_iota(jnp.int32, (vectors,), 0) < count).astype(jnp.float32)

    def apply(window_vector):
        return (window_diagonal * window_vector - coupled(window_vector, window_faces))[1:-1, 1:-1]

    def operator_input(vector):
        return extend(vector[None])[0][OV - 1 : OV + height + 1, OV - 1 : OV + breadth + 1]

    def accumulate(piece):
        return jnp.dot(coarse_inverse, piece, precision=HIGHEST_PRECISION)

    def precondition(vector_patch):
        solved = smooth(vector_patch, smooth_diagonal, faces)[OV : OV + height, OV : OV + breadth]
        flattened = vector_patch.reshape(-1)
        restricted = jnp.dot(basis, flattened, precision=HIGHEST_PRECISION) * live
        coarse = accumulate(lax.all_gather(restricted, ("gx", "gy"), axis=0, tiled=True)) * live
        spread = jnp.dot(coarse, basis, precision=HIGHEST_PRECISION)
        return solved + fold(spread.reshape(vector_patch.shape))

    source_norm = jnp.sqrt(totals(jnp.stack([jnp.sum(source * source)]))[0] + EPSILON)
    first = source / source_norm
    first_dir = precondition(source_patch / source_norm)
    image = apply(operator_input(first_dir))
    first_first = totals(jnp.stack([jnp.sum(first * image)]))[0]
    image = image - first_first * first
    second_first = jnp.sqrt(totals(jnp.stack([jnp.sum(image * image)]))[0] + EPSILON)
    second = image / second_first
    second_dir = precondition(extend(second[None])[0])
    image = apply(operator_input(second_dir))
    sums = totals(jnp.stack([jnp.sum(first * image), jnp.sum(second * image)]))
    first_second = sums[0]
    second_second = sums[1]
    image = image - first_second * first - second_second * second
    third_second = jnp.sqrt(totals(jnp.stack([jnp.sum(image * image)]))[0] + EPSILON)
    third = image / third_second
    weight_one, weight_two, remainder_one, remainder_two, remainder_three = least_squares(
        source_norm, first_first, second_first, first_second, second_second, third_second
    )
    solution = weight_one * first_dir + weight_two * second_dir
    residual = remainder_one * first + remainder_two * second + remainder_three * third
    return (solution, residual)


def solution(mesh):
    placed = (
        P("gx", "gy"),
        P("gx", "gy"),
        P("gx", "gy"),
        P("gx", "gy"),
        P("gx", "gy"),
        P("gx", "gy"),
        P("gx", "gy"),
        P(("gx", "gy"), None),
    )
    return jax.shard_map(
        on_device,
        mesh=mesh,
        in_specs=placed,
        out_specs=(P("gx", "gy"), P("gx", "gy")),
        check_vma=False,
    )
```

profile of v0, /device:TPU:0, one launch (start us, length us, event | category | flops | bytes accessed | tf_op | source)
XLA Modules:
  0.0 450.2 jit_solution(7405865456827234852)
XLA Ops:
  5.9 4.9 %collective-permute-start = (f32[5,16,256]{2,1,0:T(8,128)S(1)}, f32[5,16,256]{2,1,0:T(8,128)S(1)}, u32[]{:S(2)}, u32[]{:S(2)}) collective-permute-start(f32[5,16,256]{2,1,0:T(8,128)S(1)} %get-tuple-element.139), channel_id=1, source_target_pairs={{0,16},{1,17},{2,18},{3,19},{4,20},{5,21},{6,22},{7,23},{8,24},{9,... | collective-permute-start | bytes 245768 | tf_op jit(solution)/shard_map/ppermute | solution.py:23
  14.3 3.0 collective-permute-start.2
  17.3 42.8 %psum.35 = f32[1]{0:T(128)} all-reduce(f32[1]{0:T(128)} %bitcast), channel_id=1, replica_groups=mesh['gx'=2,'gy'=16] {'gx','gy'}, use_global_device_ids=true, to_apply=%region_1.2 | all-reduce | flops 1 | bytes 8 | tf_op jit(solution)/shard_map/psum | solution.py:93
  68.6 1.9 fusion.5
  70.8 40.3 %all-reduce.76 = f32[1024]{0:T(1024)S(1)} all-reduce(f32[1024]{0:T(1024)S(1)} %dynamic-update-slice.24), channel_id=1, replica_groups=mesh['gx'=2,'gy'=16] {'gx','gy'}, use_global_device_ids=true, to_apply=%add.76 | all-reduce | flops 1024 | bytes 8192
  116.0 4.8 %collective-permute-start.4 = (f32[16,288]{1,0:T(8,128)}, f32[16,288]{1,0:T(8,128)}, u32[]{:S(2)}, u32[]{:S(2)}) collective-permute-start(f32[16,288]{1,0:T(8,128)} %slice.692), channel_id=1, source_target_pairs={{0,16},{1,17},{2,18},{3,19},{4,20},{5,21},{6,22},{7,23},{8,24},{9,... | collective-permute-start | bytes 55304 | tf_op jit(solution)/shard_map/ppermute | solution.py:23
  126.4 1.4 slice.695
  129.9 3.9 collective-permute-done.5
  135.7 1.7 pad_add_fusion.1
  140.9 1.6 collective-permute-done.7
  144.6 1.4 collective-permute-start.9
  146.0 4.5 %collective-permute-start.8 = (f32[1,16,256]{2,1,0:T(8,128)S(1)}, f32[1,16,256]{2,1,0:T(8,128)S(1)}, u32[]{:S(2)}, u32[]{:S(2)}) collective-permute-start(f32[1,16,256]{2,1,0:T(8,128)S(1)} %get-tuple-element.221), channel_id=1, source_target_pairs={{0,16},{1,17},{2,18},{3,19},{4,20},{5,21},{6,22},{7,23},{8,24},{9,... | collective-permute-start | bytes 49160 | tf_op jit(solution)/shard_map/ppermute | solution.py:23
  150.6 1.4 collective-permute-done.8
  153.4 3.9 collective-permute-start.10
  159.7 44.4 %psum.36 = f32[]{:T(128)} all-reduce(f32[]{:T(128)} %get-tuple-element.103), channel_id=1, replica_groups=mesh['gx'=2,'gy'=16] {'gx','gy'}, use_global_device_ids=true, to_apply=%region_4.5 | all-reduce | flops 1 | bytes 8 | tf_op jit(solution)/shard_map/psum | solution.py:93
  205.4 41.3 %psum.37 = f32[1]{0:T(128)} all-reduce(f32[1]{0:T(128)} %bitcast.26), channel_id=1, replica_groups=mesh['gx'=2,'gy'=16] {'gx','gy'}, use_global_device_ids=true, to_apply=%region_6.7 | all-reduce | flops 1 | bytes 8 | tf_op jit(solution)/shard_map/psum | solution.py:93
  249.3 4.5 %collective-permute-start.12 = (f32[1,16,256]{2,1,0:T(8,128)S(1)}, f32[1,16,256]{2,1,0:T(8,128)S(1)}, u32[]{:S(2)}, u32[]{:S(2)}) collective-permute-start(f32[1,16,256]{2,1,0:T(8,128)S(1)} %get-tuple-element.219), channel_id=1, source_target_pairs={{0,16},{1,17},{2,18},{3,19},{4,20},{5,21},{6,22},{7,23},{8,24},{9,... | collective-permute-start | bytes 49160 | tf_op jit(solution)/shard_map/ppermute | solution.py:23
  253.9 1.4 collective-permute-done.12
  256.7 3.2 collective-permute-start.14
  265.7 1.9 fusion.2
  267.8 43.5 %all-reduce.77 = f32[1024]{0:T(1024)S(1)} all-reduce(f32[1024]{0:T(1024)S(1)} %dynamic-update-slice.25), channel_id=1, replica_groups=mesh['gx'=2,'gy'=16] {'gx','gy'}, use_global_device_ids=true, to_apply=%add.77 | all-reduce | flops 1024 | bytes 8192
  313.8 4.8 %collective-permute-start.16 = (f32[16,288]{1,0:T(8,128)S(1)}, f32[16,288]{1,0:T(8,128)}, u32[]{:S(2)}, u32[]{:S(2)}) collective-permute-start(f32[16,288]{1,0:T(8,128)S(1)} %slice.748), channel_id=1, source_target_pairs={{0,16},{1,17},{2,18},{3,19},{4,20},{5,21},{6,22},{7,23},{8,24},{9,... | collective-permute-start | bytes 55304 | tf_op jit(solution)/shard_map/ppermute | solution.py:23
  323.5 3.7 collective-permute-done.17
  331.9 1.6 collective-permute-done.19
  335.3 4.5 %collective-permute-start.20 = (f32[1,16,256]{2,1,0:T(8,128)S(1)}, f32[1,16,256]{2,1,0:T(8,128)S(1)}, u32[]{:S(2)}, u32[]{:S(2)}) collective-permute-start(f32[1,16,256]{2,1,0:T(8,128)S(1)} %get-tuple-element.217), channel_id=1, source_target_pairs={{0,16},{1,17},{2,18},{3,19},{4,20},{5,21},{6,22},{7,23},{8,24},{9,... | collective-permute-start | bytes 49160 | tf_op jit(solution)/shard_map/ppermute | solution.py:23
  339.9 1.4 collective-permute-done.20
  342.7 3.9 collective-permute-start.22
  350.0 2.2 multiply_reduce_fusion.2
  353.6 43.4 %psum.38 = f32[2]{0:T(128)S(1)} all-reduce(f32[2]{0:T(128)S(1)} %pad_maximum_fusion.6), channel_id=1, replica_groups=mesh['gx'=2,'gy'=16] {'gx','gy'}, use_global_device_ids=true, to_apply=%region_9.10 | all-reduce | flops 2 | bytes 16 | tf_op jit(solution)/shard_map/psum | solution.py:93
  400.2 2.6 multiply_reduce_fusion
  402.8 41.3 %psum.39 = f32[1]{0:T(128)} all-reduce(f32[1]{0:T(128)} %bitcast.41), channel_id=1, replica_groups=mesh['gx'=2,'gy'=16] {'gx','gy'}, use_global_device_ids=true, to_apply=%region_11.12 | all-reduce | flops 1 | bytes 8 | tf_op jit(solution)/shard_map/psum | solution.py:93
  447.6 2.6 multiply_add_fusion
  (185 shorter events, 69.4 us)
Async XLA Ops:
  0.6 68.0 %copy-start = (f32[32,18432]{1,0:T(8,128)S(1)}, f32[32,18432]{1,0:T(8,128)}, u32[]{:S(2)}) copy-start(f32[32,18432]{1,0:T(8,128)} %param.30) | copy-start | bytes 7077892
  4.6 7.6 %collective-permute-start.1 = (f32[5,16,256]{2,1,0:T(8,128)S(1)}, f32[5,16,256]{2,1,0:T(8,128)S(1)}, u32[]{:S(2)}, u32[]{:S(2)}) collective-permute-start(f32[5,16,256]{2,1,0:T(8,128)S(1)} %get-tuple-element.140), channel_id=1, source_target_pairs={{16,0},{17,1},{18,2},{19,3},{20,4},{21,5},{22,6},{23,7},{24,8},{25... | collective-permute-start | bytes 245768 | tf_op jit(solution)/shard_map/ppermute | solution.py:25
  5.9 6.9 %collective-permute-start = (f32[5,16,256]{2,1,0:T(8,128)S(1)}, f32[5,16,256]{2,1,0:T(8,128)S(1)}, u32[]{:S(2)}, u32[]{:S(2)}) collective-permute-start(f32[5,16,256]{2,1,0:T(8,128)S(1)} %get-tuple-element.139), channel_id=1, source_target_pairs={{0,16},{1,17},{2,18},{3,19},{4,20},{5,21},{6,22},{7,23},{8,24},{9,... | collective-permute-start | bytes 245768 | tf_op jit(solution)/shard_map/ppermute | solution.py:23
  13.0 49.2 %collective-permute-start.3 = (f32[5,64,16]{2,1,0:T(8,128)S(1)}, f32[5,64,16]{2,1,0:T(8,128)S(1)}, u32[]{:S(2)}, u32[]{:S(2)}) collective-permute-start(f32[5,64,16]{2,1,0:T(8,128)S(1)} %get-tuple-element.134), channel_id=1, source_target_pairs={{1,0},{2,1},{3,2},{4,3},{5,4},{6,5},{7,6},{8,7},{9,8},{10,9},{11,1... | collective-permute-start | bytes 61448 | tf_op jit(solution)/shard_map/ppermute | solution.py:25
  14.3 47.9 %collective-permute-start.2 = (f32[5,64,16]{2,1,0:T(8,128)S(1)}, f32[5,64,16]{2,1,0:T(8,128)S(1)}, u32[]{:S(2)}, u32[]{:S(2)}) collective-permute-start(f32[5,64,16]{2,1,0:T(8,128)S(1)} %get-tuple-element.133), channel_id=1, source_target_pairs={{0,1},{1,2},{2,3},{3,4},{4,5},{5,6},{6,7},{7,8},{8,9},{9,10},{10,1... | collective-permute-start | bytes 61448 | tf_op jit(solution)/shard_map/ppermute | solution.py:23
  62.8 3.7 copy-start.3
  116.0 13.1 %collective-permute-start.4 = (f32[16,288]{1,0:T(8,128)}, f32[16,288]{1,0:T(8,128)}, u32[]{:S(2)}, u32[]{:S(2)}) collective-permute-start(f32[16,288]{1,0:T(8,128)} %slice.692), channel_id=1, source_target_pairs={{0,16},{1,17},{2,18},{3,19},{4,20},{5,21},{6,22},{7,23},{8,24},{9,... | collective-permute-start | bytes 55304 | tf_op jit(solution)/shard_map/ppermute | solution.py:23
  122.7 36.3 %copy-start.2 = (f32[32,256]{1,0:T(8,128)S(1)}, f32[32,256]{1,0:T(8,128)}, u32[]{:S(2)}) copy-start(f32[32,256]{1,0:T(8,128)} %param.24) | copy-start | bytes 98308
  127.9 5.9 %collective-permute-start.5 = (f32[16,288]{1,0:T(8,128)}, f32[16,288]{1,0:T(8,128)S(1)}, u32[]{:S(2)}, u32[]{:S(2)}) collective-permute-start(f32[16,288]{1,0:T(8,128)} %slice.695), channel_id=1, source_target_pairs={{16,0},{17,1},{18,2},{19,3},{20,4},{21,5},{22,6},{23,7},{24,8},{25... | collective-permute-start | bytes 55304 | tf_op jit(solution)/shard_map/ppermute | solution.py:25
  134.4 4.3 collective-permute-start.6
  137.4 5.1 %collective-permute-start.7 = (f32[32,16]{1,0:T(8,128)}, f32[32,16]{1,0:T(8,128)}, u32[]{:S(2)}, u32[]{:S(2)}) collective-permute-start(f32[32,16]{1,0:T(8,128)} %get-tuple-element.215), channel_id=1, source_target_pairs={{1,0},{2,1},{3,2},{4,3},{5,4},{6,5},{7,6},{8,7},{9,8},{10,9},{11,1... | collective-permute-start | bytes 6152 | tf_op jit(solution)/shard_map/ppermute | solution.py:25
  144.6 116.0 %copy-start.4 = (f32[64,288]{1,0:T(8,128)S(1)}, f32[64,288]{1,0:T(8,128)}, u32[]{:S(2)}) copy-start(f32[64,288]{1,0:T(8,128)} %copy-done.3) | copy-start | bytes 221188
  144.6 6.0 %collective-permute-start.9 = (f32[1,16,256]{2,1,0:T(8,128)S(1)}, f32[1,16,256]{2,1,0:T(8,128)S(1)}, u32[]{:S(2)}, u32[]{:S(2)}) collective-permute-start(f32[1,16,256]{2,1,0:T(8,128)S(1)} %get-tuple-element.222), channel_id=1, source_target_pairs={{16,0},{17,1},{18,2},{19,3},{20,4},{21,5},{22,6},{23,7},{24,8},{25... | collective-permute-start | bytes 49160 | tf_op jit(solution)/shard_map/ppermute | solution.py:25
  146.0 6.0 %collective-permute-start.8 = (f32[1,16,256]{2,1,0:T(8,128)S(1)}, f32[1,16,256]{2,1,0:T(8,128)S(1)}, u32[]{:S(2)}, u32[]{:S(2)}) collective-permute-start(f32[1,16,256]{2,1,0:T(8,128)S(1)} %get-tuple-element.221), channel_id=1, source_target_pairs={{0,16},{1,17},{2,18},{3,19},{4,20},{5,21},{6,22},{7,23},{8,24},{9,... | collective-permute-start | bytes 49160 | tf_op jit(solution)/shard_map/ppermute | solution.py:23
  152.1 5.3 %collective-permute-start.11 = (f32[1,64,16]{2,1,0:T(8,128)S(1)}, f32[1,64,16]{2,1,0:T(8,128)S(1)}, u32[]{:S(2)}, u32[]{:S(2)}) collective-permute-start(f32[1,64,16]{2,1,0:T(8,128)S(1)} %get-tuple-element.212), channel_id=1, source_target_pairs={{1,0},{2,1},{3,2},{4,3},{5,4},{6,5},{7,6},{8,7},{9,8},{10,9},{11,1... | collective-permute-start | bytes 12296 | tf_op jit(solution)/shard_map/ppermute | solution.py:25
  153.4 4.7 %collective-permute-start.10 = (f32[1,64,16]{2,1,0:T(8,128)S(1)}, f32[1,64,16]{2,1,0:T(8,128)S(1)}, u32[]{:S(2)}, u32[]{:S(2)}) collective-permute-start(f32[1,64,16]{2,1,0:T(8,128)S(1)} %get-tuple-element.211), channel_id=1, source_target_pairs={{0,1},{1,2},{2,3},{3,4},{4,5},{5,6},{6,7},{7,8},{8,9},{9,10},{10,1... | collective-permute-start | bytes 12296 | tf_op jit(solution)/shard_map/ppermute | solution.py:23
  248.0 5.9 %collective-permute-start.13 = (f32[1,16,256]{2,1,0:T(8,128)S(1)}, f32[1,16,256]{2,1,0:T(8,128)S(1)}, u32[]{:S(2)}, u32[]{:S(2)}) collective-permute-start(f32[1,16,256]{2,1,0:T(8,128)S(1)} %get-tuple-element.220), channel_id=1, source_target_pairs={{16,0},{17,1},{18,2},{19,3},{20,4},{21,5},{22,6},{23,7},{24,8},{25... | collective-permute-start | bytes 49160 | tf_op jit(solution)/shard_map/ppermute | solution.py:25
  249.3 6.0 %collective-permute-start.12 = (f32[1,16,256]{2,1,0:T(8,128)S(1)}, f32[1,16,256]{2,1,0:T(8,128)S(1)}, u32[]{:S(2)}, u32[]{:S(2)}) collective-permute-start(f32[1,16,256]{2,1,0:T(8,128)S(1)} %get-tuple-element.219), channel_id=1, source_target_pairs={{0,16},{1,17},{2,18},{3,19},{4,20},{5,21},{6,22},{7,23},{8,24},{9,... | collective-permute-start | bytes 49160 | tf_op jit(solution)/shard_map/ppermute | solution.py:23
  255.4 4.5 %collective-permute-start.15 = (f32[1,64,16]{2,1,0:T(8,128)S(1)}, f32[1,64,16]{2,1,0:T(8,128)S(1)}, u32[]{:S(2)}, u32[]{:S(2)}) collective-permute-start(f32[1,64,16]{2,1,0:T(8,128)S(1)} %get-tuple-element.210), channel_id=1, source_target_pairs={{1,0},{2,1},{3,2},{4,3},{5,4},{6,5},{7,6},{8,7},{9,8},{10,9},{11,1... | collective-permute-start | bytes 12296 | tf_op jit(solution)/shard_map/ppermute | solution.py:25
  256.7 3.9 collective-permute-start.14
  263.9 1.8 copy-start.14
  313.7 4.9 %copy-start.11 = (f32[1,18432]{1,0:T(1,128)}, f32[1,18432]{1,0:T(1,128)S(1)}, u32[]{:S(2)}) copy-start(f32[1,18432]{1,0:T(1,128)S(1)} %fusion.53) | copy-start | bytes 221188
  313.7 36.1 %copy-start.6 = (f32[33,258]{1,0:T(8,128)S(1)}, f32[33,258]{1,0:T(8,128)}, u32[]{:S(2)}) copy-start(f32[33,258]{1,0:T(8,128)} %copy-done.5) | copy-start | bytes 102172
  313.7 36.1 %copy-start.8 = (f32[33,258]{1,0:T(8,128)S(1)}, f32[33,258]{1,0:T(8,128)}, u32[]{:S(2)}) copy-start(f32[33,258]{1,0:T(8,128)} %copy-done.7) | copy-start | bytes 102172
  313.8 9.0 %collective-permute-start.16 = (f32[16,288]{1,0:T(8,128)S(1)}, f32[16,288]{1,0:T(8,128)}, u32[]{:S(2)}, u32[]{:S(2)}) collective-permute-start(f32[16,288]{1,0:T(8,128)S(1)} %slice.748), channel_id=1, source_target_pairs={{0,16},{1,17},{2,18},{3,19},{4,20},{5,21},{6,22},{7,23},{8,24},{9,... | collective-permute-start | bytes 55304 | tf_op jit(solution)/shard_map/ppermute | solution.py:23
  321.5 5.7 %collective-permute-start.17 = (f32[16,288]{1,0:T(8,128)S(1)}, f32[16,288]{1,0:T(8,128)S(1)}, u32[]{:S(2)}, u32[]{:S(2)}) collective-permute-start(f32[16,288]{1,0:T(8,128)S(1)} %slice.751), channel_id=1, source_target_pairs={{16,0},{17,1},{18,2},{19,3},{20,4},{21,5},{22,6},{23,7},{24,8},{25... | collective-permute-start | bytes 55304 | tf_op jit(solution)/shard_map/ppermute | solution.py:25
  327.3 3.6 collective-permute-start.18
  329.6 4.0 collective-permute-start.19
  334.0 5.9 %collective-permute-start.21 = (f32[1,16,256]{2,1,0:T(8,128)S(1)}, f32[1,16,256]{2,1,0:T(8,128)S(1)}, u32[]{:S(2)}, u32[]{:S(2)}) collective-permute-start(f32[1,16,256]{2,1,0:T(8,128)S(1)} %get-tuple-element.218), channel_id=1, source_target_pairs={{16,0},{17,1},{18,2},{19,3},{20,4},{21,5},{22,6},{23,7},{24,8},{25... | collective-permute-start | bytes 49160 | tf_op jit(solution)/shard_map/ppermute | solution.py:25
  335.3 6.0 %collective-permute-start.20 = (f32[1,16,256]{2,1,0:T(8,128)S(1)}, f32[1,16,256]{2,1,0:T(8,128)S(1)}, u32[]{:S(2)}, u32[]{:S(2)}) collective-permute-start(f32[1,16,256]{2,1,0:T(8,128)S(1)} %get-tuple-element.217), channel_id=1, source_target_pairs={{0,16},{1,17},{2,18},{3,19},{4,20},{5,21},{6,22},{7,23},{8,24},{9,... | collective-permute-start | bytes 49160 | tf_op jit(solution)/shard_map/ppermute | solution.py:23
  341.4 7.3 %collective-permute-start.23 = (f32[1,64,16]{2,1,0:T(8,128)S(1)}, f32[1,64,16]{2,1,0:T(8,128)S(1)}, u32[]{:S(2)}, u32[]{:S(2)}) collective-permute-start(f32[1,64,16]{2,1,0:T(8,128)S(1)} %get-tuple-element.208), channel_id=1, source_target_pairs={{1,0},{2,1},{3,2},{4,3},{5,4},{6,5},{7,6},{8,7},{9,8},{10,9},{11,1... | collective-permute-start | bytes 12296 | tf_op jit(solution)/shard_map/ppermute | solution.py:25
  342.7 6.0 %collective-permute-start.22 = (f32[1,64,16]{2,1,0:T(8,128)S(1)}, f32[1,64,16]{2,1,0:T(8,128)S(1)}, u32[]{:S(2)}, u32[]{:S(2)}) collective-permute-start(f32[1,64,16]{2,1,0:T(8,128)S(1)} %get-tuple-element.207), channel_id=1, source_target_pairs={{0,1},{1,2},{2,3},{3,4},{4,5},{5,6},{6,7},{7,8},{8,9},{9,10},{10,1... | collective-permute-start | bytes 12296 | tf_op jit(solution)/shard_map/ppermute | solution.py:23
  (8 other events, 7.7 us)
where the time goes:
time: 453 us; the launch traced here: 450 us
  blocking collectives  297 us (66%)
  starting transfers between devices  60.2 us (13%)
  other arithmetic  38.2 us (8%)
  local copies, waits for them, and re-layouts  18.2 us (4%)
  waiting for transfers between devices  17.1 us (4%)
  between operations  11.1 us (2%)
  matrix products  8.54 us (2%)
    psum x5, blocking collectives, totals(): return lax.psum(values, ('gx', 'gy'))  213 us
    unnamed x2, blocking collectives  83.7 us
    ppermute x12, starting transfers between devices, padded(): lax.ppermute(tail, axis, [(i, (i + 1) % count) for i in range(ends)])  44.6 us
    ppermute x12, starting transfers between devices, padded(): lax.ppermute(head, axis, [((i + 1) % count, i) for i in range(ends)])  15.6 us
    ppermute x12, waiting for transfers between devices, padded(): lax.ppermute(head, axis, [((i + 1) % count, i) for i in range(ends)])  10.8 us
  transfers between devices with their start and end apart: 24, of which 10 were waited for; matrix products, arithmetic and copies ran while one was open for 4% of the time, Pallas kernels for 0%

commit v1 on v0

v1 whole, which is shorter than its diff:
```python
import functools
import math
import jax
import jax.numpy as jnp
from jax import lax
from jax.experimental import pallas as pl
from jax.experimental.pallas import tpu as pltpu
from jax.sharding import PartitionSpec as P

OV = 16
SWEEPS = 8
OMEGA = 0.8
EPSILON = 1e-06
LANES = 128
ROWS = 24
SIDE = 64
MESH = pl.DeviceIdType.MESH

NEAR = [(i, j) for i in (-1, 0, 1) for j in (-1, 0, 1) if (i, j) != (0, 0)]
FAR = [(i, j) for i in (-2, 2) for j in (-1, 0, 1)]


def least_squares(
    source_norm, first_first, second_first, first_second, second_second, third_second
):
    radius = jnp.sqrt(first_first * first_first + second_first * second_first)
    cosine = first_first / radius
    sine = second_first / radius
    upper_right = cosine * first_second + sine * second_second
    lower_right = cosine * second_second - sine * first_second
    radius_two = jnp.sqrt(lower_right * lower_right + third_second * third_second)
    weight_two = lower_right / radius_two * (-sine * source_norm) / radius_two
    weight_one = (cosine * source_norm - upper_right * weight_two) / radius
    remainder_one = source_norm - first_first * weight_one - first_second * weight_two
    remainder_two = -second_first * weight_one - second_second * weight_two
    remainder_three = -third_second * weight_two
    return (weight_one, weight_two, remainder_one, remainder_two, remainder_three)


def part_slices(di, dj, height, breadth):
    high, wide = height + 2 * ROWS, breadth + 2 * SIDE
    margin = ROWS - OV
    if di == 0:
        start, size, to = margin, height + 2 * OV, margin
    elif di == 1:
        start, size = height, ROWS + OV
        to = 0
    elif di == -1:
        size = ROWS + OV
        start, to = margin, high - size
    elif di == 2:
        start, size, to = 2 * height, margin, 0
    else:
        start, size, to = margin, margin, high - margin
    if dj == 0:
        lane, width, lane_to = 0, wide, 0
    elif dj == 1:
        lane, width, lane_to = wide - LANES, LANES, 0
    else:
        lane, width, lane_to = 0, LANES, wide - LANES
    return (pl.ds(start, size), pl.ds(lane, width), pl.ds(to, size), pl.ds(lane_to, width))


def kernel(
    gx, gy, far,
    counts, source, potential, along, across, recombination, basis_hbm, inverse_hbm,
    solution_out, residual_out,
    basis, inverse, grown, fields, pack_out, pack_in, part, total, flat, row_out, gathered,
    *rest,
):
    directions = NEAR + far
    arrived = rest[: len(directions)]
    load_sem, send_sem, recv_sem, row_send, row_recv = rest[len(directions):]
    devices = gx * gy
    x = lax.axis_index("gx")
    y = lax.axis_index("gy")
    me = x * gy + y
    height, breadth = source.shape
    vectors = basis.shape[0]
    high, wide = height + 2 * ROWS, breadth + 2 * SIDE
    px, py = height + 2 * OV, breadth + 2 * OV
    group = LANES // math.gcd(py, LANES)
    lines, length = px // group, py * group
    own_rows = pl.ds(ROWS, height)

    load_basis = pltpu.make_async_copy(basis_hbm, basis, load_sem.at[0])
    load_inverse = pltpu.make_async_copy(inverse_hbm, inverse, load_sem.at[1])
    load_basis.start()
    load_inverse.start()

    grown[...] = jnp.zeros_like(grown)
    fields[...] = jnp.zeros_like(fields)
    pack_in[...] = jnp.zeros_like(pack_in)
    for ref in arrived:
        ref[...] = jnp.zeros_like(ref)

    barrier = pltpu.get_barrier_semaphore()

    def greet(step, carry):
        other = lax.rem(me + step, devices)
        pl.semaphore_signal(
            barrier, inc=1, device_id=(other // gy, lax.rem(other, gy)), device_id_type=MESH
        )
        return carry

    lax.fori_loop(1, devices, greet, 0)

    grown[own_rows, pl.ds(LANES, breadth)] = source[...]
    own_fields = [potential[...], jnp.sqrt(along[...]), jnp.sqrt(across[...]), recombination[...]]
    lane = lax.broadcasted_iota(jnp.int32, (height, LANES), 1)
    strip = LANES // 4
    to_east = jnp.zeros((height, LANES), jnp.float32)
    to_west = jnp.zeros((height, LANES), jnp.float32)
    for f in range(4):
        fields[f, own_rows, :] = own_fields[f]
        here = (lane >= f * strip) & (lane < (f + 1) * strip)
        east = pltpu.roll(own_fields[f][:, breadth - LANES:], ((f + 1) * strip) % LANES, 1)
        west = pltpu.roll(own_fields[f][:, :LANES], f * strip, 1)
        to_east = jnp.where(here, east, to_east)
        to_west = jnp.where(here, west, to_west)
    pack_out[0] = to_east
    pack_out[1] = to_west

    pl.semaphore_wait(barrier, devices - 1)

    def present(di, dj):
        return (x + di >= 0) & (x + di < gx) & (y + dj >= 0) & (y + dj < gy)

    def copy(src, dst, phase, number, di, dj):
        return pltpu.make_async_remote_copy(
            src_ref=src,
            dst_ref=dst,
            send_sem=send_sem.at[phase, number],
            recv_sem=recv_sem.at[phase, number],
            device_id=(x + di, y + dj),
            device_id_type=MESH,
        )

    def source_copy(number, di, dj):
        start, size, to = {0: (0, height, ROWS), 1: (height - OV, OV, ROWS - OV), -1: (0, OV, ROWS + height)}[di]
        column, width, column_to = {
            0: (0, breadth, LANES),
            1: (breadth - LANES, LANES, 0),
            -1: (0, LANES, LANES + breadth),
        }[dj]
        return copy(
            grown.at[pl.ds(ROWS + start, size), pl.ds(LANES + column, width)],
            grown.at[pl.ds(to, size), pl.ds(column_to, width)],
            0, number, di, dj,
        )

    def field_copy(number, di, dj):
        start, size, to = {0: (0, height, ROWS), 1: (height - ROWS, ROWS, 0), -1: (0, ROWS, ROWS + height)}[di]
        if dj == 0:
            src = fields.at[:, pl.ds(ROWS + start, size), :]
            dst = fields.at[:, pl.ds(to, size), :]
        else:
            side = 0 if dj == 1 else 1
            src = pack_out.at[side, pl.ds(start, size), :]
            dst = pack_in.at[side, pl.ds(to, size), :]
        return copy(src, dst, 1, number, di, dj)

    def part_copy(turn):
        def make(number, di, dj):
            rows, columns, _, _ = part_slices(di, dj, height, breadth)
            return copy(
                part.at[turn, rows, columns], arrived[number].at[turn], 2 + turn, number, di, dj
            )

        return make

    def start_all(make, chosen):
        for number, (di, dj) in enumerate(chosen):
            @pl.when(present(di, dj))
            def _(number=number, di=di, dj=dj):
                make(number, di, dj).start()

    def receive_all(make, chosen):
        for number, (di, dj) in enumerate(chosen):
            @pl.when(present(-di, -dj))
            def _(number=number, di=di, dj=dj):
                make(number, di, dj).wait_recv()

    def sent_all(make, chosen):
        for number, (di, dj) in enumerate(chosen):
            @pl.when(present(di, dj))
            def _(number=number, di=di, dj=dj):
                make(number, di, dj).wait_send()

    def share(turn):
        def send(step, carry):
            other = lax.rem(me + step, devices)
            pltpu.make_async_remote_copy(
                src_ref=row_out.at[turn],
                dst_ref=gathered.at[turn, me],
                send_sem=row_send.at[turn],
                recv_sem=row_recv.at[turn],
                device_id=(other // gy, lax.rem(other, gy)),
                device_id_type=MESH,
            ).start()
            return carry

        gathered[turn, me] = row_out[turn]
        lax.fori_loop(1, devices, send, 0)

    def row_bytes(turn, sem):
        some = gathered.at[turn, pl.ds(0, devices - 1)]
        return pltpu.make_async_copy(some, some, sem.at[turn])

    def collect(turn):
        row_bytes(turn, row_recv).wait()
        return gathered[turn].reshape(devices, LANES)

    start_all(source_copy, NEAR)
    start_all(field_copy, NEAR)

    frame_row = lax.broadcasted_iota(jnp.int32, (high, wide), 0)
    frame_lane = lax.broadcasted_iota(jnp.int32, (high, wide), 1)
    grid_row = frame_row - ROWS + x * height
    grid_lane = frame_lane - SIDE + y * breadth
    inside = (
        (grid_row >= 0) & (grid_row < height * gx) & (grid_lane >= 0) & (grid_lane < breadth * gy)
    )
    own = (
        (frame_row >= ROWS) & (frame_row < ROWS + height)
        & (frame_lane >= SIDE) & (frame_lane < SIDE + breadth)
    )
    line_lane = lax.broadcasted_iota(jnp.int32, (lines, wide), 1)
    in_patch = (line_lane >= SIDE - OV) & (line_lane < SIDE + breadth + OV)
    vector_index = lax.broadcasted_iota(jnp.int32, (vectors, 1), 0)
    live = (vector_index < counts[0, 0]).astype(jnp.float32)
    quarter = lax.rem(me, 4)
    row_lane = lax.broadcasted_iota(jnp.int32, (1, LANES), 1)
    spot = (
        lax.broadcasted_iota(jnp.int32, (vectors, LANES), 1)
        == lax.broadcasted_iota(jnp.int32, (vectors, LANES), 0) + strip * quarter
    )
    device_row = lax.broadcasted_iota(jnp.int32, (devices, LANES), 0)
    device_lane = lax.broadcasted_iota(jnp.int32, (devices, LANES), 1)
    is_coarse = device_lane // strip == lax.rem(device_row, 4)

    def restrict():
        pieces = None
        for q in range(group):
            taken = jnp.concatenate(
                [
                    total[t, pl.ds(ROWS - OV + q, lines, stride=group), :]
                    for t in range(wide // LANES)
                ],
                axis=1,
            )
            taken = jnp.where(in_patch, taken, 0.0)
            taken = jnp.concatenate(
                [taken, jnp.zeros((lines, length - wide), jnp.float32)], axis=1
            )
            taken = pltpu.roll(taken, (py * q - (SIDE - OV)) % length, 1)
            pieces = taken if pieces is None else pieces + taken
        flat[...] = pieces
        summed = jnp.zeros((vectors, length), jnp.float32)
        for a in range(lines):
            summed = summed + basis[:, a * length:(a + 1) * length] * flat[a:a + 1, :]
        folded = summed[:, :LANES]
        for t in range(1, length // LANES):
            folded = folded + summed[:, t * LANES:(t + 1) * LANES]
        coarse = jnp.sum(folded, axis=1, keepdims=True) * live
        return jnp.sum(jnp.where(spot, coarse, 0.0), axis=0, keepdims=True)

    def spread(rows):
        rows = jnp.where(is_coarse, rows, 0.0)
        joined = rows
        for i in range(1, 4):
            joined = joined + pltpu.roll(rows, i, 0)
        summed = jnp.zeros((vectors, LANES), jnp.float32)
        for b in range(devices // 4):
            summed = (
                summed + inverse[:, b * LANES:(b + 1) * LANES] * joined[4 * b + 3:4 * b + 4, :]
            )
        weights = jnp.sum(summed, axis=1, keepdims=True) * live
        weights = jnp.broadcast_to(weights, (vectors, LANES))
        weights = jnp.concatenate([weights] * (length // LANES), axis=1)
        for a in range(lines):
            flat[a:a + 1, :] = jnp.sum(
                basis[:, a * length:(a + 1) * length] * weights, axis=0, keepdims=True
            )
        whole = flat[...]
        for t in range(wide // LANES):
            total[t] = jnp.zeros((high, LANES), jnp.float32)
        for q in range(group):
            moved = pltpu.roll(whole, (SIDE - OV - py * q) % length, 1)[:, :wide]
            moved = jnp.where(in_patch, moved, 0.0)
            for t in range(wide // LANES):
                total[t, pl.ds(ROWS - OV + q, lines, stride=group), :] = (
                    moved[:, t * LANES:(t + 1) * LANES]
                )
        return get_total()

    def set_total(value):
        for t in range(wide // LANES):
            total[t] = value[:, t * LANES:(t + 1) * LANES]

    def get_total():
        return jnp.concatenate([total[t] for t in range(wide // LANES)], axis=1)

    def around(value):
        return (
            pltpu.roll(value, high - 1, 0),
            pltpu.roll(value, 1, 0),
            pltpu.roll(value, wide - 1, 1),
            pltpu.roll(value, 1, 1),
        )

    def exchange(turn, value):
        part[turn] = value
        start_all(part_copy(turn), directions)
        receive_all(part_copy(turn), directions)
        set_total(value)
        for number, (di, dj) in enumerate(directions):
            _, _, rows, columns = part_slices(di, dj, height, breadth)
            got = arrived[number][turn]
            first = columns.start // LANES
            for t in range(columns.size // LANES):
                total[first + t, rows, :] = (
                    total[first + t, rows, :] + got[:, t * LANES:(t + 1) * LANES]
                )
        return jnp.where(inside, get_total(), 0.0)

    def dots(pairs):
        row = jnp.zeros((1, LANES), jnp.float32)
        place = lax.rem(quarter + 1, 4) * strip
        for i, (one, other) in enumerate(pairs):
            product = jnp.sum(jnp.where(own, one * other, 0.0), axis=0, keepdims=True)
            value = jnp.sum(product, axis=1, keepdims=True)
            row = jnp.where(row_lane == place + i, value, row)
        return row

    def whole_sums(rows, count):
        others = jnp.where(is_coarse, 0.0, rows)
        row = jnp.sum(others, axis=0, keepdims=True)
        return [
            jnp.sum(jnp.where(lax.rem(row_lane, strip) == i, row, 0.0), axis=1, keepdims=True)
            for i in range(count)
        ]

    receive_all(source_copy, NEAR)
    first_vector = pltpu.roll(grown[...], wide + LANES - SIDE, 1)[:, :wide]
    set_total(first_vector)
    load_basis.wait()
    row_out[0] = restrict()
    share(0)

    receive_all(field_copy, NEAR)
    patch = []
    side_lane = lax.broadcasted_iota(jnp.int32, (high, LANES), 1)
    for f in range(4):
        base = jnp.concatenate([fields[f], jnp.zeros((high, LANES), jnp.float32)], axis=1)
        base = pltpu.roll(base, SIDE, 1)
        west = pltpu.roll(pack_in[0], (SIDE - (f + 1) * strip) % LANES, 1)
        east = pltpu.roll(pack_in[1], (SIDE - f * strip) % LANES, 1)
        left = jnp.where((side_lane >= SIDE - strip) & (side_lane < SIDE), west, base[:, :LANES])
        right = jnp.where(
            (side_lane >= SIDE) & (side_lane < SIDE + strip), east, base[:, wide - LANES:]
        )
        patch.append(jnp.concatenate([left, base[:, LANES:wide - LANES], right], axis=1))
    level = jnp.exp(0.5 * patch[0])
    level_inverse = jnp.exp(-0.5 * patch[0])
    root_along, root_across = patch[1], patch[2]
    faces = (
        root_along * pltpu.roll(root_along, high - 1, 0),
        root_along * pltpu.roll(root_along, 1, 0),
        root_across * pltpu.roll(root_across, wide - 1, 1),
        root_across * pltpu.roll(root_across, 1, 1),
    )
    outflow = jnp.zeros((high, wide), jnp.float32)
    for face, beside in zip(faces, around(level_inverse)):
        outflow = outflow + face * beside
    diagonal = patch[3] + level * outflow
    diagonal = jnp.where(diagonal > 0.0, diagonal, 1.0)
    step_size = OMEGA / diagonal
    step_faces = [face * step_size for face in faces]
    step_level = step_size * level

    def smooth(vector):
        scaled = step_level * vector
        field = scaled
        for sweep in range(SWEEPS - 1):
            moved = (1.0 - OMEGA) * field + scaled
            for face, beside in zip(step_faces, around(field)):
                moved = moved + face * beside
            field = moved
        return jnp.where(own, level_inverse * field, 0.0)

    def apply(vector):
        scaled = level * vector
        image = diagonal * scaled
        for face, beside in zip(faces, around(scaled)):
            image = image - face * beside
        return level_inverse * image

    solved = smooth(first_vector)
    load_inverse.wait()
    first_dir = exchange(0, solved + spread(collect(0)))
    image = apply(first_dir)

    set_total(image)
    row_out[1] = restrict() + dots(
        [(first_vector, first_vector), (first_vector, image), (image, image)]
    )
    share(1)
    solved = smooth(image)
    rows = collect(1)
    second_dir = exchange(1, solved + spread(rows))
    squares, mixed, image_squares = whole_sums(rows, 3)
    source_norm = jnp.sqrt(squares + EPSILON)
    shrink = 1.0 / source_norm
    first_first = mixed * shrink * shrink
    left_over = (
        image_squares * shrink * shrink
        - 2.0 * first_first * first_first
        + first_first * first_first * (squares * shrink * shrink)
    )
    second_first = jnp.sqrt(jnp.maximum(left_over, 0.0) + EPSILON)
    first = first_vector * shrink
    first_dir = first_dir * shrink
    second = (image * shrink - first_first * first) / second_first
    second_dir = (second_dir * shrink - first_first * first_dir) / second_first
    image = apply(second_dir)
    row_out[2] = dots(
        [(first, image), (second, image), (image, image), (first, first), (second, second),
         (first, second)]
    )
    share(2)
    first_second, second_second, image_squares, ones, twos, cross = whole_sums(collect(2), 6)
    left_over = (
        image_squares
        - 2.0 * (first_second * first_second + second_second * second_second)
        + first_second * first_second * ones
        + second_second * second_second * twos
        + 2.0 * first_second * second_second * cross
    )
    third_second = jnp.sqrt(jnp.maximum(left_over, 0.0) + EPSILON)
    image = image - first_second * first - second_second * second
    weight_one, weight_two, remainder_one, remainder_two, remainder_three = least_squares(
        source_norm, first_first, second_first, first_second, second_second, third_second
    )
    answer = weight_one * first_dir + weight_two * second_dir
    remainder = (
        remainder_one * first + remainder_two * second + (remainder_three / third_second) * image
    )
    solution_out[...] = pltpu.roll(answer[ROWS:ROWS + height], wide - SIDE, 1)[:, :breadth]
    residual_out[...] = pltpu.roll(remainder[ROWS:ROWS + height], wide - SIDE, 1)[:, :breadth]

    sent_all(source_copy, NEAR)
    sent_all(field_copy, NEAR)
    for turn in range(2):
        sent_all(part_copy(turn), directions)
    for turn in range(3):
        row_bytes(turn, row_send).wait()


def on_device(
    gx, gy,
    source, potential, mobility_along, mobility_across, recombination, counts, basis, coarse_inverse
):
    height, breadth = source.shape
    vectors = basis.shape[0]
    devices = gx * gy
    high, wide = height + 2 * ROWS, breadth + 2 * SIDE
    px, py = height + 2 * OV, breadth + 2 * OV
    group = LANES // math.gcd(py, LANES)
    far = FAR if gx > 2 else []
    arrived = []
    for di, dj in NEAR + far:
        rows, columns, _, _ = part_slices(di, dj, height, breadth)
        arrived.append(pltpu.VMEM((2, rows.size, columns.size), jnp.float32))
    vmem = pl.BlockSpec(memory_space=pltpu.VMEM)
    hbm = pl.BlockSpec(memory_space=pl.ANY)
    ways = len(arrived)
    return pl.pallas_call(
        functools.partial(kernel, gx, gy, far),
        out_shape=(
            jax.ShapeDtypeStruct((height, breadth), jnp.float32),
            jax.ShapeDtypeStruct((height, breadth), jnp.float32),
        ),
        in_specs=[pl.BlockSpec(memory_space=pltpu.SMEM)] + [vmem] * 5 + [hbm] * 2,
        out_specs=(vmem, vmem),
        scratch_shapes=[
            pltpu.VMEM(basis.shape, jnp.float32),
            pltpu.VMEM(coarse_inverse.shape, jnp.float32),
            pltpu.VMEM((high, breadth + 2 * LANES), jnp.float32),
            pltpu.VMEM((4, high, breadth), jnp.float32),
            pltpu.VMEM((2, height, LANES), jnp.float32),
            pltpu.VMEM((2, high, LANES), jnp.float32),
            pltpu.VMEM((2, high, wide), jnp.float32),
            pltpu.VMEM((wide // LANES, high, LANES), jnp.float32),
            pltpu.VMEM((px // group, py * group), jnp.float32),
            pltpu.VMEM((3, 1, LANES), jnp.float32),
            pltpu.VMEM((3, devices, 1, LANES), jnp.float32),
            *arrived,
            pltpu.SemaphoreType.DMA((2,)),
            pltpu.SemaphoreType.DMA((4, ways)),
            pltpu.SemaphoreType.DMA((4, ways)),
            pltpu.SemaphoreType.DMA((3,)),
            pltpu.SemaphoreType.DMA((3,)),
        ],
        compiler_params=pltpu.CompilerParams(
            collective_id=0, has_side_effects=True, vmem_limit_bytes=32 * 1024 * 1024
        ),
    )(counts, source, potential, mobility_along, mobility_across, recombination, basis, coarse_inverse)


def solution(mesh):
    placed = (P("gx", "gy"),) * 7 + (P(("gx", "gy"), None),)
    return jax.shard_map(
        functools.partial(on_device, mesh.shape["gx"], mesh.shape["gy"]),
        mesh=mesh,
        in_specs=placed,
        out_specs=(P("gx", "gy"), P("gx", "gy")),
        check_vma=False,
    )
```

time: 453 us -> 42.5 us (0.09)
  blocking collectives: 297 us -> 0 us
  starting transfers between devices: 60.2 us -> 0 us
  other arithmetic: 38.2 us -> 0 us
  Pallas kernels: 0 us -> 33.1 us
  waiting for transfers between devices: 17.1 us -> 0 us
  local copies, waits for them, and re-layouts: 18.2 us -> 7.58 us
  between operations: 11.1 us -> 1.3 us
  matrix products: 8.54 us -> 0 us
    psum x5 -> x0, blocking collectives: 213 us -> none  [totals(): return lax.psum(values, ('gx', 'gy'))]
    unnamed x2 -> x0, blocking collectives: 83.7 us -> none
    ppermute x24 -> x0, starting transfers between devices: 60.2 us -> none  [the longest x12 44.6 us: padded(): lax.ppermute(tail, axis, [(i, (i + 1) % count) for i in range(ends)])]
    pallas_call x0 -> x1, Pallas kernels: none -> 33.1 us  [on_device(): pl.pallas_call(functools.partial(kernel, gx, gy, far), out_shape=(jax.Sha...]
    ppermute x24 -> x0, waiting for transfers between devices: 17.1 us -> none  [the longest x12 10.8 us: padded(): lax.ppermute(head, axis, [((i + 1) % count, i) for i in range(ends)])]
    add x21 -> x0, other arithmetic: 13.2 us -> none  [the longest x12 5.31 us: smooth(): field + OMEGA * (vector_patch - (diagonal * field - coupled(field, faces)...]
    mul x34 -> x0, other arithmetic: 9.77 us -> none  [the longest x17 5.73 us: coupled(): total = total + jnp.pad(eastward * field[:, 1:], ((0, 0), (0, 1)))]
    slice x25 -> x0, local copies, waits for them, and re-layouts: 8.7 us -> none  [the longest x6 3.6 us: fold(): edges = jnp.concatenate([part[:OV], part[-OV:]], axis=0)]
  transfers between devices with their start and end apart: 24 -> 0, of which waited for: 10 -> 0; matrix products, arithmetic and copies ran while one was open for 4% -> 0% of each run, Pallas kernels for 0% -> 0%
where the time goes in v1:
time: 42.5 us; the launch traced here: 42 us
  Pallas kernels  33.1 us (78%)
  local copies, waits for them, and re-layouts  7.58 us (18%)
  between operations  1.3 us (3%)
    pallas_call x1, Pallas kernels, on_device(): pl.pallas_call(functools.partial(kernel, gx, gy, far), out_shape=(jax.Sha...  33.1 us
    unnamed x16, local copies, waits for them, and re-layouts  7.58 us

profile of v1, /device:TPU:0, one launch (start us, length us, event | category | flops | bytes accessed | tf_op | source)
XLA Modules:
  0.0 42.0 jit_solution(9286115636168264229)
XLA Ops:
  1.3 0.0 copy-start
  1.3 1.7 %copy-done = f32[32,18432]{1,0:T(8,128)S(1)} copy-done((f32[32,18432]{1,0:T(8,128)S(1)}, f32[32,18432]{1,0:T(8,128)}, u32[]{:S(2)}) %copy-start) | copy-done | bytes 2359320
  2.9 0.0 copy-start.1
  2.9 0.9 %copy-done.1 = f32[32,1024]{1,0:T(8,128)S(1)} copy-done((f32[32,1024]{1,0:T(8,128)S(1)}, f32[32,1024]{1,0:T(8,128)}, u32[]{:S(2)}) %copy-start.1) | copy-done | bytes 131096
  3.8 0.0 copy-start.2
  3.9 0.8 %copy-done.2 = f32[32,256]{1,0:T(8,128)S(1)} copy-done((f32[32,256]{1,0:T(8,128)S(1)}, f32[32,256]{1,0:T(8,128)}, u32[]{:S(2)}) %copy-start.2) | copy-done | bytes 32792
  4.6 0.0 copy-start.3
  4.6 0.8 %copy-done.3 = f32[32,256]{1,0:T(8,128)S(1)} copy-done((f32[32,256]{1,0:T(8,128)S(1)}, f32[32,256]{1,0:T(8,128)}, u32[]{:S(2)}) %copy-start.3) | copy-done | bytes 32792
  5.4 0.0 copy-start.4
  5.4 0.8 %copy-done.4 = f32[32,256]{1,0:T(8,128)S(1)} copy-done((f32[32,256]{1,0:T(8,128)S(1)}, f32[32,256]{1,0:T(8,128)}, u32[]{:S(2)}) %copy-start.4) | copy-done | bytes 32792
  6.1 0.0 copy-start.5
  6.1 0.8 %copy-done.5 = f32[32,256]{1,0:T(8,128)S(1)} copy-done((f32[32,256]{1,0:T(8,128)S(1)}, f32[32,256]{1,0:T(8,128)}, u32[]{:S(2)}) %copy-start.5) | copy-done | bytes 32792
  6.9 0.0 copy-start.6
  6.9 0.8 %copy-done.6 = f32[32,256]{1,0:T(8,128)S(1)} copy-done((f32[32,256]{1,0:T(8,128)S(1)}, f32[32,256]{1,0:T(8,128)}, u32[]{:S(2)}) %copy-start.6) | copy-done | bytes 32792
  7.6 33.1 %shard_map.95 = (f32[32,256]{1,0:T(8,128)S(1)}, f32[32,256]{1,0:T(8,128)S(1)}) custom-call(s32[1,1]{1,0:T(1,128)S(6)} %copy.12.counts, f32[32,256]{1,0:T(8,128)S(1)} %copy-done.2, f32[32,256]{1,0:T(8,128)S(1)} %copy-done.3, f32[32,256]{1,0:T(8,128)S(1)} %copy-done.4, f32[32,256]{1,0:T(8,128)S(1)} %copy-done.5, f32[32,256]{1,0:T(8,128)S(1)} %copy-done.6, ...), custom_call_target="tpu_custom_call" | custom-call | tf_op jit(solution)/shard_map/pallas_call | solution.py:478
  40.7 0.6 %copy.13 = f32[32,256]{1,0:T(8,128)} copy(f32[32,256]{1,0:T(8,128)S(1)} %get-tuple-element.4) | data formatting | bytes 65536
  41.4 0.6 %copy.14 = f32[32,256]{1,0:T(8,128)} copy(f32[32,256]{1,0:T(8,128)S(1)} %get-tuple-element.5) | data formatting | bytes 65536
Async XLA Ops:
  1.3 1.7 %copy-start = (f32[32,18432]{1,0:T(8,128)S(1)}, f32[32,18432]{1,0:T(8,128)}, u32[]{:S(2)}) copy-start(f32[32,18432]{1,0:T(8,128)} %basis_hbm.1) | copy-start | bytes 7077892
  2.9 0.9 %copy-start.1 = (f32[32,1024]{1,0:T(8,128)S(1)}, f32[32,1024]{1,0:T(8,128)}, u32[]{:S(2)}) copy-start(f32[32,1024]{1,0:T(8,128)} %inverse_hbm.1) | copy-start | bytes 393220
  3.8 0.8 %copy-start.2 = (f32[32,256]{1,0:T(8,128)S(1)}, f32[32,256]{1,0:T(8,128)}, u32[]{:S(2)}) copy-start(f32[32,256]{1,0:T(8,128)} %source.1) | copy-start | bytes 98308
  4.6 0.8 %copy-start.3 = (f32[32,256]{1,0:T(8,128)S(1)}, f32[32,256]{1,0:T(8,128)}, u32[]{:S(2)}) copy-start(f32[32,256]{1,0:T(8,128)} %potential.1) | copy-start | bytes 98308
  5.4 0.8 %copy-start.4 = (f32[32,256]{1,0:T(8,128)S(1)}, f32[32,256]{1,0:T(8,128)}, u32[]{:S(2)}) copy-start(f32[32,256]{1,0:T(8,128)} %along.1) | copy-start | bytes 98308
  6.1 0.8 %copy-start.5 = (f32[32,256]{1,0:T(8,128)S(1)}, f32[32,256]{1,0:T(8,128)}, u32[]{:S(2)}) copy-start(f32[32,256]{1,0:T(8,128)} %across.1) | copy-start | bytes 98308
  6.9 0.8 %copy-start.6 = (f32[32,256]{1,0:T(8,128)S(1)}, f32[32,256]{1,0:T(8,128)}, u32[]{:S(2)}) copy-start(f32[32,256]{1,0:T(8,128)} %recombination.1) | copy-start | bytes 98308

commit v2 on v1

--- a/solution.py
+++ b/solution.py
@@ -14,6 +14,7 @@
 LANES = 128
 ROWS = 24
 SIDE = 64
+NARROW = 8
 MESH = pl.DeviceIdType.MESH
 
 NEAR = [(i, j) for i in (-1, 0, 1) for j in (-1, 0, 1) if (i, j) != (0, 0)]
@@ -37,17 +38,17 @@
     return (weight_one, weight_two, remainder_one, remainder_two, remainder_three)
 
 
-def part_slices(di, dj, height, breadth):
+def part_slices(turn, di, dj, height, breadth):
     high, wide = height + 2 * ROWS, breadth + 2 * SIDE
     margin = ROWS - OV
+    reach = ROWS if turn == 0 else NARROW
     if di == 0:
-        start, size, to = margin, height + 2 * OV, margin
+        used = min(reach, OV)
+        start, size, to = ROWS - used, height + 2 * used, ROWS - used
     elif di == 1:
-        start, size = height, ROWS + OV
-        to = 0
+        start, size, to = height + ROWS - reach, reach + OV, ROWS - reach
     elif di == -1:
-        size = ROWS + OV
-        start, to = margin, high - size
+        start, size, to = margin, reach + OV, ROWS + height - OV
     elif di == 2:
         start, size, to = 2 * height, margin, 0
     else:
@@ -63,14 +64,14 @@
 
 def kernel(
     gx, gy, far,
-    counts, source, potential, along, across, recombination, basis_hbm, inverse_hbm,
+    counts_hbm, source, potential, along, across, recombination, basis_hbm, inverse_hbm,
     solution_out, residual_out,
-    basis, inverse, grown, fields, pack_out, pack_in, part, total, flat, row_out, gathered,
-    *rest,
+    counts, basis, inverse, grown, raw, fields, pack_out, pack_in, part, total, flat, row_out,
+    gathered, *rest,
 ):
-    directions = NEAR + far
-    arrived = rest[: len(directions)]
-    load_sem, send_sem, recv_sem, row_send, row_recv = rest[len(directions):]
+    directions = (NEAR + far, NEAR)
+    arrived = (rest[: len(directions[0])], rest[len(directions[0]):][: len(NEAR)])
+    load_sem, send_sem, recv_sem, row_send, row_recv = rest[len(directions[0]) + len(NEAR):]
     devices = gx * gy
     x = lax.axis_index("gx")
     y = lax.axis_index("gy")
@@ -83,45 +84,45 @@
     lines, length = px // group, py * group
     own_rows = pl.ds(ROWS, height)
 
-    load_basis = pltpu.make_async_copy(basis_hbm, basis, load_sem.at[0])
-    load_inverse = pltpu.make_async_copy(inverse_hbm, inverse, load_sem.at[1])
-    load_basis.start()
-    load_inverse.start()
-
-    grown[...] = jnp.zeros_like(grown)
-    fields[...] = jnp.zeros_like(fields)
-    pack_in[...] = jnp.zeros_like(pack_in)
-    for ref in arrived:
-        ref[...] = jnp.zeros_like(ref)
-
+    def wrapped(place, step, size):
+        return jnp.where(place + step >= size, place + step - size, place + step)
+
+    few = devices <= 64
+    along_x = [wrapped(x, a, gx) if a else x for a in range(gx)]
+    along_y = [wrapped(y, b, gy) if b else y for b in range(gy)] if few else []
+
+    def to_others(act):
+        for a in range(gx):
+            if few:
+                for b in range(gy):
+                    if a or b:
+                        act((along_x[a], along_y[b]))
+            else:
+                def step(b, carry, a=a):
+                    act((along_x[a], wrapped(y, b, gy)))
+                    return carry
+
+                lax.fori_loop(0 if a else 1, gy, step, 0)
+
+    sources = [
+        (source, grown.at[own_rows, pl.ds(LANES, breadth)]),
+        (potential, fields.at[0, own_rows, :]),
+        (along, raw.at[0]),
+        (across, raw.at[1]),
+        (recombination, fields.at[3, own_rows, :]),
+        (counts_hbm, counts),
+        (inverse_hbm, inverse),
+        (basis_hbm, basis),
+    ]
+    loads = [
+        pltpu.make_async_copy(src, dst, load_sem.at[i]) for i, (src, dst) in enumerate(sources)
+    ]
+    for load in loads:
+        load.start()
     barrier = pltpu.get_barrier_semaphore()
-
-    def greet(step, carry):
-        other = lax.rem(me + step, devices)
-        pl.semaphore_signal(
-            barrier, inc=1, device_id=(other // gy, lax.rem(other, gy)), device_id_type=MESH
-        )
-        return carry
-
-    lax.fori_loop(1, devices, greet, 0)
-
-    grown[own_rows, pl.ds(LANES, breadth)] = source[...]
-    own_fields = [potential[...], jnp.sqrt(along[...]), jnp.sqrt(across[...]), recombination[...]]
-    lane = lax.broadcasted_iota(jnp.int32, (height, LANES), 1)
-    strip = LANES // 4
-    to_east = jnp.zeros((height, LANES), jnp.float32)
-    to_west = jnp.zeros((height, LANES), jnp.float32)
-    for f in range(4):
-        fields[f, own_rows, :] = own_fields[f]
-        here = (lane >= f * strip) & (lane < (f + 1) * strip)
-        east = pltpu.roll(own_fields[f][:, breadth - LANES:], ((f + 1) * strip) % LANES, 1)
-        west = pltpu.roll(own_fields[f][:, :LANES], f * strip, 1)
-        to_east = jnp.where(here, east, to_east)
-        to_west = jnp.where(here, west, to_west)
-    pack_out[0] = to_east
-    pack_out[1] = to_west
-
-    pl.semaphore_wait(barrier, devices - 1)
+    to_others(
+        lambda place: pl.semaphore_signal(barrier, inc=1, device_id=place, device_id_type=MESH)
+    )
 
     def present(di, dj):
         return (x + di >= 0) & (x + di < gx) & (y + dj >= 0) & (y + dj < gy)
@@ -136,35 +137,46 @@
             device_id_type=MESH,
         )
 
-    def source_copy(number, di, dj):
-        start, size, to = {0: (0, height, ROWS), 1: (height - OV, OV, ROWS - OV), -1: (0, OV, ROWS + height)}[di]
+    def source_target(di, dj):
+        start, size, to = {
+            0: (0, height, ROWS),
+            1: (height - OV, OV, ROWS - OV),
+            -1: (0, OV, ROWS + height),
+        }[di]
         column, width, column_to = {
             0: (0, breadth, LANES),
             1: (breadth - LANES, LANES, 0),
             -1: (0, LANES, LANES + breadth),
         }[dj]
-        return copy(
+        return (
             grown.at[pl.ds(ROWS + start, size), pl.ds(LANES + column, width)],
             grown.at[pl.ds(to, size), pl.ds(column_to, width)],
-            0, number, di, dj,
         )
 
+    def field_target(di, dj):
+        start, size, to = {
+            0: (0, height, ROWS),
+            1: (height - ROWS, ROWS, 0),
+            -1: (0, ROWS, ROWS + height),
+        }[di]
+        if dj == 0:
+            return (
+                fields.at[:, pl.ds(ROWS + start, size), :], fields.at[:, pl.ds(to, size), :]
+            )
+        side = 0 if dj == 1 else 1
+        return (pack_out.at[side, pl.ds(start, size), :], pack_in.at[side, pl.ds(to, size), :])
+
+    def source_copy(number, di, dj):
+        return copy(*source_target(di, dj), 0, number, di, dj)
+
     def field_copy(number, di, dj):
-        start, size, to = {0: (0, height, ROWS), 1: (height - ROWS, ROWS, 0), -1: (0, ROWS, ROWS + height)}[di]
-        if dj == 0:
-            src = fields.at[:, pl.ds(ROWS + start, size), :]
-            dst = fields.at[:, pl.ds(to, size), :]
-        else:
-            side = 0 if dj == 1 else 1
-            src = pack_out.at[side, pl.ds(start, size), :]
-            dst = pack_in.at[side, pl.ds(to, size), :]
-        return copy(src, dst, 1, number, di, dj)
+        return copy(*field_target(di, dj), 1, number, di, dj)
 
     def part_copy(turn):
         def make(number, di, dj):
-            rows, columns, _, _ = part_slices(di, dj, height, breadth)
+            rows, columns, _, _ = part_slices(turn, di, dj, height, breadth)
             return copy(
-                part.at[turn, rows, columns], arrived[number].at[turn], 2 + turn, number, di, dj
+                part.at[turn, rows, columns], arrived[turn][number], 2 + turn, number, di, dj
             )
 
         return make
@@ -188,20 +200,17 @@
                 make(number, di, dj).wait_send()
 
     def share(turn):
-        def send(step, carry):
-            other = lax.rem(me + step, devices)
-            pltpu.make_async_remote_copy(
+        gathered[turn, me] = row_out[turn]
+        to_others(
+            lambda place: pltpu.make_async_remote_copy(
                 src_ref=row_out.at[turn],
                 dst_ref=gathered.at[turn, me],
                 send_sem=row_send.at[turn],
                 recv_sem=row_recv.at[turn],
-                device_id=(other // gy, lax.rem(other, gy)),
+                device_id=place,
                 device_id_type=MESH,
             ).start()
-            return carry
-
-        gathered[turn, me] = row_out[turn]
-        lax.fori_loop(1, devices, send, 0)
+        )
 
     def row_bytes(turn, sem):
         some = gathered.at[turn, pl.ds(0, devices - 1)]
@@ -211,8 +220,43 @@
         row_bytes(turn, row_recv).wait()
         return gathered[turn].reshape(devices, LANES)
 
+    for number, (di, dj) in enumerate(directions[0]):
+        @pl.when(jnp.logical_not(present(-di, -dj)))
+        def _(number=number, di=di, dj=dj):
+            targets = [arrived[0][number]]
+            if (di, dj) in NEAR:
+                targets += [
+                    arrived[1][number], source_target(di, dj)[1], field_target(di, dj)[1]
+                ]
+            for target in targets:
+                target[...] = jnp.zeros(target.shape, jnp.float32)
+
+    unused = jnp.zeros((ROWS - OV, breadth + 2 * LANES), jnp.float32)
+    grown[: ROWS - OV, :] = unused
+    grown[high - ROWS + OV:, :] = unused
+
+    loads[0].wait()
+    pl.semaphore_wait(barrier, devices - 1)
     start_all(source_copy, NEAR)
+
+    for load in loads[1:5]:
+        load.wait()
+    fields[1, own_rows, :] = jnp.sqrt(raw[0])
+    fields[2, own_rows, :] = jnp.sqrt(raw[1])
+    lane = lax.broadcasted_iota(jnp.int32, (height, LANES), 1)
+    strip = LANES // 4
+    to_east = jnp.zeros((height, LANES), jnp.float32)
+    to_west = jnp.zeros((height, LANES), jnp.float32)
+    for f in range(4):
+        here = (lane >= f * strip) & (lane < (f + 1) * strip)
+        east = fields[f, own_rows, breadth - LANES:]
+        west = fields[f, own_rows, :LANES]
+        to_east = jnp.where(here, pltpu.roll(east, ((f + 1) * strip) % LANES, 1), to_east)
+        to_west = jnp.where(here, pltpu.roll(west, f * strip, 1), to_west)
+    pack_out[0] = to_east
+    pack_out[1] = to_west
     start_all(field_copy, NEAR)
+    loads[5].wait()
 
     frame_row = lax.broadcasted_iota(jnp.int32, (high, wide), 0)
     frame_lane = lax.broadcasted_iota(jnp.int32, (high, wide), 1)
@@ -221,10 +265,8 @@
     inside = (
         (grid_row >= 0) & (grid_row < height * gx) & (grid_lane >= 0) & (grid_lane < breadth * gy)
     )
-    own = (
-        (frame_row >= ROWS) & (frame_row < ROWS + height)
-        & (frame_lane >= SIDE) & (frame_lane < SIDE + breadth)
-    )
+    own_lane = lax.broadcasted_iota(jnp.int32, (height, wide), 1)
+    own = (own_lane >= SIDE) & (own_lane < SIDE + breadth)
     line_lane = lax.broadcasted_iota(jnp.int32, (lines, wide), 1)
     in_patch = (line_lane >= SIDE - OV) & (line_lane < SIDE + breadth + OV)
     vector_index = lax.broadcasted_iota(jnp.int32, (vectors, 1), 0)
@@ -302,21 +344,21 @@
         return jnp.concatenate([total[t] for t in range(wide // LANES)], axis=1)
 
     def around(value):
+        rows = value.shape[0]
         return (
-            pltpu.roll(value, high - 1, 0),
+            pltpu.roll(value, rows - 1, 0),
             pltpu.roll(value, 1, 0),
             pltpu.roll(value, wide - 1, 1),
             pltpu.roll(value, 1, 1),
         )
 
-    def exchange(turn, value):
-        part[turn] = value
-        start_all(part_copy(turn), directions)
-        receive_all(part_copy(turn), directions)
-        set_total(value)
-        for number, (di, dj) in enumerate(directions):
-            _, _, rows, columns = part_slices(di, dj, height, breadth)
-            got = arrived[number][turn]
+    def exchange(turn):
+        start_all(part_copy(turn), directions[turn])
+        set_total(part[turn])
+        receive_all(part_copy(turn), directions[turn])
+        for number, (di, dj) in enumerate(directions[turn]):
+            _, _, rows, columns = part_slices(turn, di, dj, height, breadth)
+            got = arrived[turn][number][...]
             first = columns.start // LANES
             for t in range(columns.size // LANES):
                 total[first + t, rows, :] = (
@@ -344,7 +386,7 @@
     receive_all(source_copy, NEAR)
     first_vector = pltpu.roll(grown[...], wide + LANES - SIDE, 1)[:, :wide]
     set_total(first_vector)
-    load_basis.wait()
+    loads[7].wait()
     row_out[0] = restrict()
     share(0)
 
@@ -375,40 +417,56 @@
         outflow = outflow + face * beside
     diagonal = patch[3] + level * outflow
     diagonal = jnp.where(diagonal > 0.0, diagonal, 1.0)
-    step_size = OMEGA / diagonal
-    step_faces = [face * step_size for face in faces]
-    step_level = step_size * level
+    near = slice(ROWS - NARROW, ROWS + height + NARROW)
+    middle = slice(NARROW, NARROW + height)
+    mine = slice(ROWS, ROWS + height)
+    step_size = OMEGA / diagonal[near]
+    step_faces = [face[near] * step_size for face in faces]
+    step_level = step_size * level[near]
+    own_level_inverse = level_inverse[mine]
 
     def smooth(vector):
-        scaled = step_level * vector
+        scaled = step_level * vector[near]
         field = scaled
         for sweep in range(SWEEPS - 1):
             moved = (1.0 - OMEGA) * field + scaled
             for face, beside in zip(step_faces, around(field)):
                 moved = moved + face * beside
             field = moved
-        return jnp.where(own, level_inverse * field, 0.0)
-
-    def apply(vector):
-        scaled = level * vector
-        image = diagonal * scaled
+        return jnp.where(own, own_level_inverse * field[middle], 0.0)
+
+    def apply(vector, rows):
+        scaled = level[rows] * vector
+        image = diagonal[rows] * scaled
         for face, beside in zip(faces, around(scaled)):
-            image = image - face * beside
-        return level_inverse * image
+            image = image - face[rows] * beside
+        return level_inverse[rows] * image
+
+    def put_part(turn, solved, spreads):
+        part[turn] = spreads
+        part[turn, own_rows, :] = spreads[mine] + solved
 
     solved = smooth(first_vector)
-    load_inverse.wait()
-    first_dir = exchange(0, solved + spread(collect(0)))
-    image = apply(first_dir)
+    loads[6].wait()
+    put_part(0, solved, spread(collect(0)))
+    first_dir = exchange(0)
+    image = apply(first_dir, slice(0, high))
 
     set_total(image)
+    first_vector_own, image_own = first_vector[mine], image[mine]
     row_out[1] = restrict() + dots(
-        [(first_vector, first_vector), (first_vector, image), (image, image)]
+        [
+            (first_vector_own, first_vector_own),
+            (first_vector_own, image_own),
+            (image_own, image_own),
+        ]
     )
     share(1)
     solved = smooth(image)
     rows = collect(1)
-    second_dir = exchange(1, solved + spread(rows))
+    put_part(1, solved, spread(rows))
+    second_dir = exchange(1)[near]
+    first_dir, first_vector, image = first_dir[near], first_vector[near], image[near]
     squares, mixed, image_squares = whole_sums(rows, 3)
     source_norm = jnp.sqrt(squares + EPSILON)
     shrink = 1.0 / source_norm
@@ -423,7 +481,9 @@
     first_dir = first_dir * shrink
     second = (image * shrink - first_first * first) / second_first
     second_dir = (second_dir * shrink - first_first * first_dir) / second_first
-    image = apply(second_dir)
+    image = apply(second_dir, near)[middle]
+    first_dir, second_dir = first_dir[middle], second_dir[middle]
+    first, second = first[middle], second[middle]
     row_out[2] = dots(
         [(first, image), (second, image), (image, image), (first, first), (second, second),
          (first, second)]
@@ -446,13 +506,13 @@
     remainder = (
         remainder_one * first + remainder_two * second + (remainder_three / third_second) * image
     )
-    solution_out[...] = pltpu.roll(answer[ROWS:ROWS + height], wide - SIDE, 1)[:, :breadth]
-    residual_out[...] = pltpu.roll(remainder[ROWS:ROWS + height], wide - SIDE, 1)[:, :breadth]
+    solution_out[...] = pltpu.roll(answer, wide - SIDE, 1)[:, :breadth]
+    residual_out[...] = pltpu.roll(remainder, wide - SIDE, 1)[:, :breadth]
 
     sent_all(source_copy, NEAR)
     sent_all(field_copy, NEAR)
     for turn in range(2):
-        sent_all(part_copy(turn), directions)
+        sent_all(part_copy(turn), directions[turn])
     for turn in range(3):
         row_bytes(turn, row_send).wait()
 
@@ -469,24 +529,27 @@
     group = LANES // math.gcd(py, LANES)
     far = FAR if gx > 2 else []
     arrived = []
-    for di, dj in NEAR + far:
-        rows, columns, _, _ = part_slices(di, dj, height, breadth)
-        arrived.append(pltpu.VMEM((2, rows.size, columns.size), jnp.float32))
+    for turn, chosen in enumerate((NEAR + far, NEAR)):
+        for di, dj in chosen:
+            rows, columns, _, _ = part_slices(turn, di, dj, height, breadth)
+            arrived.append(pltpu.VMEM((rows.size, columns.size), jnp.float32))
     vmem = pl.BlockSpec(memory_space=pltpu.VMEM)
-    hbm = pl.BlockSpec(memory_space=pl.ANY)
-    ways = len(arrived)
+    hbm = pl.BlockSpec(memory_space=pltpu.HBM)
+    ways = len(NEAR + far)
     return pl.pallas_call(
         functools.partial(kernel, gx, gy, far),
         out_shape=(
             jax.ShapeDtypeStruct((height, breadth), jnp.float32),
             jax.ShapeDtypeStruct((height, breadth), jnp.float32),
         ),
-        in_specs=[pl.BlockSpec(memory_space=pltpu.SMEM)] + [vmem] * 5 + [hbm] * 2,
+        in_specs=[hbm] * 8,
         out_specs=(vmem, vmem),
         scratch_shapes=[
+            pltpu.SMEM((1, 1), jnp.int32),
             pltpu.VMEM(basis.shape, jnp.float32),
             pltpu.VMEM(coarse_inverse.shape, jnp.float32),
             pltpu.VMEM((high, breadth + 2 * LANES), jnp.float32),
+            pltpu.VMEM((2, height, breadth), jnp.float32),
             pltpu.VMEM((4, high, breadth), jnp.float32),
             pltpu.VMEM((2, height, LANES), jnp.float32),
             pltpu.VMEM((2, high, LANES), jnp.float32),
@@ -496,7 +559,7 @@
             pltpu.VMEM((3, 1, LANES), jnp.float32),
             pltpu.VMEM((3, devices, 1, LANES), jnp.float32),
             *arrived,
-            pltpu.SemaphoreType.DMA((2,)),
+            pltpu.SemaphoreType.DMA((8,)),
             pltpu.SemaphoreType.DMA((4, ways)),
             pltpu.SemaphoreType.DMA((4, ways)),
             pltpu.SemaphoreType.DMA((3,)),

time: 42.5 us -> 42.1 us (level)
  no operation moved by 1% of the time
where the time goes in v2:
time: 42.1 us; the launch traced here: 41.6 us
  Pallas kernels  32.7 us (78%)
  local copies, waits for them, and re-layouts  7.58 us (18%)
  between operations  1.3 us (3%)
    pallas_call x1, Pallas kernels, on_device(): pl.pallas_call(functools.partial(kernel, gx, gy, far), out_shape=(jax.Sha...  32.7 us
    unnamed x16, local copies, waits for them, and re-layouts  7.58 us

profile of v2, /device:TPU:0, one launch (start us, length us, event | category | flops | bytes accessed | tf_op | source)
XLA Modules:
  0.0 41.6 jit_solution(11839003622188910573)
XLA Ops:
  1.3 0.0 copy-start
  1.3 1.7 %copy-done = f32[32,18432]{1,0:T(8,128)S(1)} copy-done((f32[32,18432]{1,0:T(8,128)S(1)}, f32[32,18432]{1,0:T(8,128)}, u32[]{:S(2)}) %copy-start) | copy-done | bytes 2359320
  2.9 0.0 copy-start.1
  2.9 0.9 %copy-done.1 = f32[32,1024]{1,0:T(8,128)S(1)} copy-done((f32[32,1024]{1,0:T(8,128)S(1)}, f32[32,1024]{1,0:T(8,128)}, u32[]{:S(2)}) %copy-start.1) | copy-done | bytes 131096
  3.8 0.0 copy-start.2
  3.9 0.8 %copy-done.2 = f32[32,256]{1,0:T(8,128)S(1)} copy-done((f32[32,256]{1,0:T(8,128)S(1)}, f32[32,256]{1,0:T(8,128)}, u32[]{:S(2)}) %copy-start.2) | copy-done | bytes 32792
  4.6 0.0 copy-start.3
  4.6 0.8 %copy-done.3 = f32[32,256]{1,0:T(8,128)S(1)} copy-done((f32[32,256]{1,0:T(8,128)S(1)}, f32[32,256]{1,0:T(8,128)}, u32[]{:S(2)}) %copy-start.3) | copy-done | bytes 32792
  5.4 0.0 copy-start.4
  5.4 0.8 %copy-done.4 = f32[32,256]{1,0:T(8,128)S(1)} copy-done((f32[32,256]{1,0:T(8,128)S(1)}, f32[32,256]{1,0:T(8,128)}, u32[]{:S(2)}) %copy-start.4) | copy-done | bytes 32792
  6.1 0.0 copy-start.5
  6.1 0.8 %copy-done.5 = f32[32,256]{1,0:T(8,128)S(1)} copy-done((f32[32,256]{1,0:T(8,128)S(1)}, f32[32,256]{1,0:T(8,128)}, u32[]{:S(2)}) %copy-start.5) | copy-done | bytes 32792
  6.9 0.0 copy-start.6
  6.9 0.8 %copy-done.6 = f32[32,256]{1,0:T(8,128)S(1)} copy-done((f32[32,256]{1,0:T(8,128)S(1)}, f32[32,256]{1,0:T(8,128)}, u32[]{:S(2)}) %copy-start.6) | copy-done | bytes 32792
  7.6 32.7 %shard_map.95 = (f32[32,256]{1,0:T(8,128)S(1)}, f32[32,256]{1,0:T(8,128)S(1)}) custom-call(s32[1,1]{1,0:T(1,128)S(6)} %copy.12.counts_hbm, f32[32,256]{1,0:T(8,128)S(1)} %copy-done.2, f32[32,256]{1,0:T(8,128)S(1)} %copy-done.3, f32[32,256]{1,0:T(8,128)S(1)} %copy-done.4, f32[32,256]{1,0:T(8,128)S(1)} %copy-done.5, f32[32,256]{1,0:T(8,128)S(1)} %copy-done.6, ...), custom_call_target="tpu_custom_call" | custom-call | tf_op jit(solution)/shard_map/pallas_call | solution.py:539
  40.3 0.6 %copy.13 = f32[32,256]{1,0:T(8,128)} copy(f32[32,256]{1,0:T(8,128)S(1)} %get-tuple-element.4) | data formatting | bytes 65536
  40.9 0.6 %copy.14 = f32[32,256]{1,0:T(8,128)} copy(f32[32,256]{1,0:T(8,128)S(1)} %get-tuple-element.5) | data formatting | bytes 65536
Async XLA Ops:
  1.3 1.7 %copy-start = (f32[32,18432]{1,0:T(8,128)S(1)}, f32[32,18432]{1,0:T(8,128)}, u32[]{:S(2)}) copy-start(f32[32,18432]{1,0:T(8,128)} %basis_hbm.1) | copy-start | bytes 7077892
  2.9 0.9 %copy-start.1 = (f32[32,1024]{1,0:T(8,128)S(1)}, f32[32,1024]{1,0:T(8,128)}, u32[]{:S(2)}) copy-start(f32[32,1024]{1,0:T(8,128)} %inverse_hbm.1) | copy-start | bytes 393220
  3.8 0.8 %copy-start.2 = (f32[32,256]{1,0:T(8,128)S(1)}, f32[32,256]{1,0:T(8,128)}, u32[]{:S(2)}) copy-start(f32[32,256]{1,0:T(8,128)} %source.1) | copy-start | bytes 98308
  4.6 0.8 %copy-start.3 = (f32[32,256]{1,0:T(8,128)S(1)}, f32[32,256]{1,0:T(8,128)}, u32[]{:S(2)}) copy-start(f32[32,256]{1,0:T(8,128)} %potential.1) | copy-start | bytes 98308
  5.4 0.8 %copy-start.4 = (f32[32,256]{1,0:T(8,128)S(1)}, f32[32,256]{1,0:T(8,128)}, u32[]{:S(2)}) copy-start(f32[32,256]{1,0:T(8,128)} %along.1) | copy-start | bytes 98308
  6.1 0.8 %copy-start.5 = (f32[32,256]{1,0:T(8,128)S(1)}, f32[32,256]{1,0:T(8,128)}, u32[]{:S(2)}) copy-start(f32[32,256]{1,0:T(8,128)} %across.1) | copy-start | bytes 98308
  6.9 0.8 %copy-start.6 = (f32[32,256]{1,0:T(8,128)S(1)}, f32[32,256]{1,0:T(8,128)}, u32[]{:S(2)}) copy-start(f32[32,256]{1,0:T(8,128)} %recombination.1) | copy-start | bytes 98308

commit v3 on v2

--- a/solution.py
+++ b/solution.py
@@ -15,6 +15,7 @@
 ROWS = 24
 SIDE = 64
 NARROW = 8
+VMEM_GRANT = 63 * 1024 * 1024
 MESH = pl.DeviceIdType.MESH
 
 NEAR = [(i, j) for i in (-1, 0, 1) for j in (-1, 0, 1) if (i, j) != (0, 0)]
@@ -36,6 +37,13 @@
     remainder_two = -second_first * weight_one - second_second * weight_two
     remainder_three = -third_second * weight_two
     return (weight_one, weight_two, remainder_one, remainder_two, remainder_three)
+
+
+def split(gy):
+    inner = 4
+    while 4 * inner * inner <= gy:
+        inner *= 2
+    return inner
 
 
 def part_slices(turn, di, dj, height, breadth):
@@ -71,11 +79,10 @@
 ):
     directions = (NEAR + far, NEAR)
     arrived = (rest[: len(directions[0])], rest[len(directions[0]):][: len(NEAR)])
-    load_sem, send_sem, recv_sem, row_send, row_recv = rest[len(directions[0]) + len(NEAR):]
+    load_sem, send_sem, recv_sem, row_send, row_recv, block_send, block_recv = rest[len(directions[0]) + len(NEAR):]
     devices = gx * gy
     x = lax.axis_index("gx")
     y = lax.axis_index("gy")
-    me = x * gy + y
     height, breadth = source.shape
     vectors = basis.shape[0]
     high, wide = height + 2 * ROWS, breadth + 2 * SIDE
@@ -84,25 +91,26 @@
     lines, length = px // group, py * group
     own_rows = pl.ds(ROWS, height)
 
+    inner = split(gy)
+    outer = gy // inner
+    members = gx * inner
+    which, seat = y // inner, lax.rem(y, inner)
+
     def wrapped(place, step, size):
-        return jnp.where(place + step >= size, place + step - size, place + step)
-
-    few = devices <= 64
-    along_x = [wrapped(x, a, gx) if a else x for a in range(gx)]
-    along_y = [wrapped(y, b, gy) if b else y for b in range(gy)] if few else []
-
-    def to_others(act):
-        for a in range(gx):
-            if few:
-                for b in range(gy):
-                    if a or b:
-                        act((along_x[a], along_y[b]))
-            else:
-                def step(b, carry, a=a):
-                    act((along_x[a], wrapped(y, b, gy)))
-                    return carry
-
-                lax.fori_loop(0 if a else 1, gy, step, 0)
+        return jnp.where(place + step >= size, place + step - size, place + step) if step else place
+
+    group_places = [
+        (wrapped(x, a, gx), which * inner + wrapped(seat, b, inner))
+        for a in range(gx) for b in range(inner) if a or b
+    ]
+    peer_places = [(x, wrapped(which, o, outer) * inner + seat) for o in range(1, outer)]
+    slot = which * members + x * inner + seat
+
+    def present(di, dj):
+        return (x + di >= 0) & (x + di < gx) & (y + dj >= 0) & (y + dj < gy)
+
+    def beyond(di, dj):
+        return present(di, dj) & (seat == (inner - 1 if dj == 1 else 0))
 
     sources = [
         (source, grown.at[own_rows, pl.ds(LANES, breadth)]),
@@ -120,12 +128,18 @@
     for load in loads:
         load.start()
     barrier = pltpu.get_barrier_semaphore()
-    to_others(
-        lambda place: pl.semaphore_signal(barrier, inc=1, device_id=place, device_id_type=MESH)
-    )
-
-    def present(di, dj):
-        return (x + di >= 0) & (x + di < gx) & (y + dj >= 0) & (y + dj < gy)
+    for place in group_places + peer_places:
+        pl.semaphore_signal(barrier, inc=1, device_id=place, device_id_type=MESH)
+    greeted = len(group_places) + len(peer_places)
+    for di, dj in directions[0]:
+        if dj != 0:
+            greeted = greeted + jnp.where(beyond(di, dj), 1, 0)
+
+            @pl.when(beyond(di, dj))
+            def _(di=di, dj=dj):
+                pl.semaphore_signal(
+                    barrier, inc=1, device_id=(x + di, y + dj), device_id_type=MESH
+                )
 
     def copy(src, dst, phase, number, di, dj):
         return pltpu.make_async_remote_copy(
@@ -200,24 +214,36 @@
                 make(number, di, dj).wait_send()
 
     def share(turn):
-        gathered[turn, me] = row_out[turn]
-        to_others(
-            lambda place: pltpu.make_async_remote_copy(
+        gathered[turn, slot] = row_out[turn]
+        for place in group_places:
+            pltpu.make_async_remote_copy(
                 src_ref=row_out.at[turn],
-                dst_ref=gathered.at[turn, me],
+                dst_ref=gathered.at[turn, slot],
                 send_sem=row_send.at[turn],
                 recv_sem=row_recv.at[turn],
                 device_id=place,
                 device_id_type=MESH,
             ).start()
-        )
-
-    def row_bytes(turn, sem):
-        some = gathered.at[turn, pl.ds(0, devices - 1)]
+
+    def row_bytes(turn, count, sem):
+        some = gathered.at[turn, pl.ds(0, count)]
         return pltpu.make_async_copy(some, some, sem.at[turn])
 
+    def pass_on(turn):
+        row_bytes(turn, members - 1, row_recv).wait()
+        rows = gathered.at[turn, pl.ds(which * members, members)]
+        for place in peer_places:
+            pltpu.make_async_remote_copy(
+                src_ref=rows,
+                dst_ref=rows,
+                send_sem=block_send.at[turn],
+                recv_sem=block_recv.at[turn],
+                device_id=place,
+                device_id_type=MESH,
+            ).start()
+
     def collect(turn):
-        row_bytes(turn, row_recv).wait()
+        row_bytes(turn, devices - members, block_recv).wait()
         return gathered[turn].reshape(devices, LANES)
 
     for number, (di, dj) in enumerate(directions[0]):
@@ -236,7 +262,7 @@
     grown[high - ROWS + OV:, :] = unused
 
     loads[0].wait()
-    pl.semaphore_wait(barrier, devices - 1)
+    pl.semaphore_wait(barrier, greeted)
     start_all(source_copy, NEAR)
 
     for load in loads[1:5]:
@@ -271,7 +297,7 @@
     in_patch = (line_lane >= SIDE - OV) & (line_lane < SIDE + breadth + OV)
     vector_index = lax.broadcasted_iota(jnp.int32, (vectors, 1), 0)
     live = (vector_index < counts[0, 0]).astype(jnp.float32)
-    quarter = lax.rem(me, 4)
+    quarter = lax.rem(seat, 4)
     row_lane = lax.broadcasted_iota(jnp.int32, (1, LANES), 1)
     spot = (
         lax.broadcasted_iota(jnp.int32, (vectors, LANES), 1)
@@ -314,8 +340,11 @@
             joined = joined + pltpu.roll(rows, i, 0)
         summed = jnp.zeros((vectors, LANES), jnp.float32)
         for b in range(devices // 4):
+            first = 4 * b
+            device = (first % members) // inner * gy + first // members * inner + first % inner
             summed = (
-                summed + inverse[:, b * LANES:(b + 1) * LANES] * joined[4 * b + 3:4 * b + 4, :]
+                summed
+                + inverse[:, device * strip:device * strip + LANES] * joined[first + 3:first + 4, :]
             )
         weights = jnp.sum(summed, axis=1, keepdims=True) * live
         weights = jnp.broadcast_to(weights, (vectors, LANES))
@@ -425,10 +454,12 @@
     step_level = step_size * level[near]
     own_level_inverse = level_inverse[mine]
 
-    def smooth(vector):
+    def smooth(vector, turn):
         scaled = step_level * vector[near]
         field = scaled
         for sweep in range(SWEEPS - 1):
+            if sweep == 2 * turn:
+                pass_on(turn)
             moved = (1.0 - OMEGA) * field + scaled
             for face, beside in zip(step_faces, around(field)):
                 moved = moved + face * beside
@@ -446,7 +477,7 @@
         part[turn] = spreads
         part[turn, own_rows, :] = spreads[mine] + solved
 
-    solved = smooth(first_vector)
+    solved = smooth(first_vector, 0)
     loads[6].wait()
     put_part(0, solved, spread(collect(0)))
     first_dir = exchange(0)
@@ -462,7 +493,7 @@
         ]
     )
     share(1)
-    solved = smooth(image)
+    solved = smooth(image, 1)
     rows = collect(1)
     put_part(1, solved, spread(rows))
     second_dir = exchange(1)[near]
@@ -489,6 +520,7 @@
          (first, second)]
     )
     share(2)
+    pass_on(2)
     first_second, second_second, image_squares, ones, twos, cross = whole_sums(collect(2), 6)
     left_over = (
         image_squares
@@ -514,7 +546,8 @@
     for turn in range(2):
         sent_all(part_copy(turn), directions[turn])
     for turn in range(3):
-        row_bytes(turn, row_send).wait()
+        row_bytes(turn, members - 1, row_send).wait()
+        row_bytes(turn, devices - members, block_send).wait()
 
 
 def on_device(
@@ -564,9 +597,11 @@
             pltpu.SemaphoreType.DMA((4, ways)),
             pltpu.SemaphoreType.DMA((3,)),
             pltpu.SemaphoreType.DMA((3,)),
+            pltpu.SemaphoreType.DMA((3,)),
+            pltpu.SemaphoreType.DMA((3,)),
         ],
         compiler_params=pltpu.CompilerParams(
-            collective_id=0, has_side_effects=True, vmem_limit_bytes=32 * 1024 * 1024
+            collective_id=0, has_side_effects=True, vmem_limit_bytes=VMEM_GRANT
         ),
     )(counts, source, potential, mobility_along, mobility_across, recombination, basis, coarse_inverse)
 

time: 42.1 us -> 43.9 us (1.043)
  Pallas kernels: 32.7 us -> 39.6 us
  local copies, waits for them, and re-layouts: 7.58 us -> 2.75 us
    pallas_call x1, Pallas kernels: 32.7 us -> 39.6 us  [on_device(): pl.pallas_call(functools.partial(kernel, gx, gy, far), out_shape=(jax.Sha...]
    unnamed x16 -> x2, local copies, waits for them, and re-layouts: 7.58 us -> 2.75 us
where the time goes in v3:
time: 43.9 us; the launch traced here: 43.7 us
  Pallas kernels  39.6 us (90%)
  local copies, waits for them, and re-layouts  2.75 us (6%)
  between operations  1.29 us (3%)
    pallas_call x1, Pallas kernels, on_device(): pl.pallas_call(functools.partial(kernel, gx, gy, far), out_shape=(jax.Sha...  39.6 us
    unnamed x2, local copies, waits for them, and re-layouts  2.75 us

profile of v3, /device:TPU:0, one launch (start us, length us, event | category | flops | bytes accessed | tf_op | source)
XLA Modules:
  0.0 43.7 jit_solution(1023075576209134038)
XLA Ops:
  1.3 39.6 %shard_map.95 = (f32[32,256]{1,0:T(8,128)}, f32[32,256]{1,0:T(8,128)}) custom-call(s32[1,1]{1,0:T(1,128)S(6)} %copy.12.counts_hbm, f32[32,256]{1,0:T(8,128)} %source.1, f32[32,256]{1,0:T(8,128)} %potential.1, f32[32,256]{1,0:T(8,128)} %along.1, f32[32,256]{1,0:T(8,128)} %across.1, f32[32,256]{1,0:T(8,128)} %recombination.1, f32[32,18432]{1,0:T(8,128)} %basis_hbm.1, ...), custom_call_target="tpu_custom_call" | custom-call | tf_op jit(solution)/shard_map/pallas_call | solution.py:572
  40.9 1.4 %copy.13 = f32[32,256]{1,0:T(8,128)} copy(f32[32,256]{1,0:T(8,128)} %get-tuple-element.4) | data formatting | bytes 65536
  42.3 1.4 %copy.14 = f32[32,256]{1,0:T(8,128)} copy(f32[32,256]{1,0:T(8,128)} %get-tuple-element.5) | data formatting | bytes 65536

commit v4 on v2

--- a/solution.py
+++ b/solution.py
@@ -15,6 +15,7 @@
 ROWS = 24
 SIDE = 64
 NARROW = 8
+VMEM_GRANT = 63 * 1024 * 1024
 MESH = pl.DeviceIdType.MESH
 
 NEAR = [(i, j) for i in (-1, 0, 1) for j in (-1, 0, 1) if (i, j) != (0, 0)]
@@ -65,7 +66,7 @@
 def kernel(
     gx, gy, far,
     counts_hbm, source, potential, along, across, recombination, basis_hbm, inverse_hbm,
-    solution_out, residual_out,
+    both_out,
     counts, basis, inverse, grown, raw, fields, pack_out, pack_in, part, total, flat, row_out,
     gathered, *rest,
 ):
@@ -506,8 +507,8 @@
     remainder = (
         remainder_one * first + remainder_two * second + (remainder_three / third_second) * image
     )
-    solution_out[...] = pltpu.roll(answer, wide - SIDE, 1)[:, :breadth]
-    residual_out[...] = pltpu.roll(remainder, wide - SIDE, 1)[:, :breadth]
+    both_out[0] = pltpu.roll(answer, wide - SIDE, 1)[:, :breadth]
+    both_out[1] = pltpu.roll(remainder, wide - SIDE, 1)[:, :breadth]
 
     sent_all(source_copy, NEAR)
     sent_all(field_copy, NEAR)
@@ -536,14 +537,11 @@
     vmem = pl.BlockSpec(memory_space=pltpu.VMEM)
     hbm = pl.BlockSpec(memory_space=pltpu.HBM)
     ways = len(NEAR + far)
-    return pl.pallas_call(
+    both = pl.pallas_call(
         functools.partial(kernel, gx, gy, far),
-        out_shape=(
-            jax.ShapeDtypeStruct((height, breadth), jnp.float32),
-            jax.ShapeDtypeStruct((height, breadth), jnp.float32),
-        ),
+        out_shape=jax.ShapeDtypeStruct((2, height, breadth), jnp.float32),
         in_specs=[hbm] * 8,
-        out_specs=(vmem, vmem),
+        out_specs=vmem,
         scratch_shapes=[
             pltpu.SMEM((1, 1), jnp.int32),
             pltpu.VMEM(basis.shape, jnp.float32),
@@ -566,9 +564,10 @@
             pltpu.SemaphoreType.DMA((3,)),
         ],
         compiler_params=pltpu.CompilerParams(
-            collective_id=0, has_side_effects=True, vmem_limit_bytes=32 * 1024 * 1024
+            collective_id=0, has_side_effects=True, vmem_limit_bytes=VMEM_GRANT
         ),
     )(counts, source, potential, mobility_along, mobility_across, recombination, basis, coarse_inverse)
+    return both[0], both[1]
 
 
 def solution(mesh):

time: 42.1 us -> 35.8 us (0.85)
  local copies, waits for them, and re-layouts: 7.58 us -> 1.4 us
    unnamed x16 -> x0, local copies, waits for them, and re-layouts: 7.58 us -> none
    squeeze x0 -> x1, local copies, waits for them, and re-layouts: none -> 1.4 us  [on_device(): return (both[0], both[1])]
where the time goes in v4:
time: 35.8 us; the launch traced here: 35.6 us
  Pallas kernels  32.9 us (92%)
  local copies, waits for them, and re-layouts  1.4 us (4%)
  between operations  1.29 us (4%)
    pallas_call x1, Pallas kernels, on_device(): pl.pallas_call(functools.partial(kernel, gx, gy, far), out_shape=jax.Shap...  32.9 us
    squeeze x1, local copies, waits for them, and re-layouts, on_device(): return (both[0], both[1])  1.4 us

profile of v4, /device:TPU:0, one launch (start us, length us, event | category | flops | bytes accessed | tf_op | source)
XLA Modules:
  0.0 35.6 jit_solution(4380331744644748164)
XLA Ops:
  1.3 32.9 %shard_map.95 = f32[2,32,256]{2,1,0:T(8,128)} custom-call(s32[1,1]{1,0:T(1,128)S(6)} %copy.10.counts_hbm, f32[32,256]{1,0:T(8,128)} %source.1, f32[32,256]{1,0:T(8,128)} %potential.1, f32[32,256]{1,0:T(8,128)} %along.1, f32[32,256]{1,0:T(8,128)} %across.1, f32[32,256]{1,0:T(8,128)} %recombination.1, f32[32,18432]{1,0:T(8,128)} %basis_hbm.1, ...), custom_call_target="tpu_custom_call" | custom-call | tf_op jit(solution)/shard_map/pallas_call | solution.py:540
  34.2 1.4 %slice_bitcast_fusion = (f32[32,256]{1,0:T(8,128)}, f32[32,256]{1,0:T(8,128)}) fusion(f32[2,32,256]{2,1,0:T(8,128)} %shard_map.95), kind=kLoop, calls=%fused_computation | loop fusion | bytes 131072 | tf_op jit(solution)/shard_map/squeeze | solution.py:570

commit v5 on v4

--- a/solution.py
+++ b/solution.py
@@ -20,23 +20,6 @@
 
 NEAR = [(i, j) for i in (-1, 0, 1) for j in (-1, 0, 1) if (i, j) != (0, 0)]
 FAR = [(i, j) for i in (-2, 2) for j in (-1, 0, 1)]
-
-
-def least_squares(
-    source_norm, first_first, second_first, first_second, second_second, third_second
-):
-    radius = jnp.sqrt(first_first * first_first + second_first * second_first)
-    cosine = first_first / radius
-    sine = second_first / radius
-    upper_right = cosine * first_second + sine * second_second
-    lower_right = cosine * second_second - sine * first_second
-    radius_two = jnp.sqrt(lower_right * lower_right + third_second * third_second)
-    weight_two = lower_right / radius_two * (-sine * source_norm) / radius_two
-    weight_one = (cosine * source_norm - upper_right * weight_two) / radius
-    remainder_one = source_norm - first_first * weight_one - first_second * weight_two
-    remainder_two = -second_first * weight_one - second_second * weight_two
-    remainder_three = -third_second * weight_two
-    return (weight_one, weight_two, remainder_one, remainder_two, remainder_three)
 
 
 def part_slices(turn, di, dj, height, breadth):
@@ -308,6 +291,27 @@
         coarse = jnp.sum(folded, axis=1, keepdims=True) * live
         return jnp.sum(jnp.where(spot, coarse, 0.0), axis=0, keepdims=True)
 
+    sublane = lax.broadcasted_iota(jnp.int32, (8, length), 0)
+
+    def weighted(product):
+        summed = product[:8]
+        for k in range(8, vectors, 8):
+            summed = summed + product[k:k + 8]
+        return summed
+
+    def eight_sums(pieces):
+        for distance in (4, 2, 1):
+            low = lax.rem(sublane // distance, 2) == 0
+            merged = []
+            for one, other in zip(pieces[:distance], pieces[distance:]):
+                away = jnp.where(low, other, one)
+                back = pltpu.roll(away, distance, 0)
+                if distance != 4:
+                    back = jnp.where(low, pltpu.roll(away, 8 - distance, 0), back)
+                merged.append(jnp.where(low, one, other) + back)
+            pieces = merged
+        return pieces[0]
+
     def spread(rows):
         rows = jnp.where(is_coarse, rows, 0.0)
         joined = rows
@@ -321,11 +325,16 @@
         weights = jnp.sum(summed, axis=1, keepdims=True) * live
         weights = jnp.broadcast_to(weights, (vectors, LANES))
         weights = jnp.concatenate([weights] * (length // LANES), axis=1)
-        for a in range(lines):
-            flat[a:a + 1, :] = jnp.sum(
-                basis[:, a * length:(a + 1) * length] * weights, axis=0, keepdims=True
-            )
-        whole = flat[...]
+        whole = jnp.concatenate(
+            [
+                eight_sums([
+                    weighted(basis[:, a * length:(a + 1) * length] * weights)
+                    for a in range(first, first + 8)
+                ])
+                for first in range(0, lines, 8)
+            ],
+            axis=0,
+        )
         for t in range(wide // LANES):
             total[t] = jnp.zeros((high, LANES), jnp.float32)
         for q in range(group):
@@ -353,9 +362,10 @@
             pltpu.roll(value, 1, 1),
         )
 
-    def exchange(turn):
+    def exchange(turn, meanwhile=lambda: None):
         start_all(part_copy(turn), directions[turn])
         set_total(part[turn])
+        found = meanwhile()
         receive_all(part_copy(turn), directions[turn])
         for number, (di, dj) in enumerate(directions[turn]):
             _, _, rows, columns = part_slices(turn, di, dj, height, breadth)
@@ -365,15 +375,15 @@
                 total[first + t, rows, :] = (
                     total[first + t, rows, :] + got[:, t * LANES:(t + 1) * LANES]
                 )
-        return jnp.where(inside, get_total(), 0.0)
-
-    def dots(pairs):
+        return jnp.where(inside, get_total(), 0.0), found
+
+    def dots(pairs, first=0):
         row = jnp.zeros((1, LANES), jnp.float32)
         place = lax.rem(quarter + 1, 4) * strip
         for i, (one, other) in enumerate(pairs):
             product = jnp.sum(jnp.where(own, one * other, 0.0), axis=0, keepdims=True)
             value = jnp.sum(product, axis=1, keepdims=True)
-            row = jnp.where(row_lane == place + i, value, row)
+            row = jnp.where(row_lane == place + first + i, value, row)
         return row
 
     def whole_sums(rows, count):
@@ -450,7 +460,7 @@
     solved = smooth(first_vector)
     loads[6].wait()
     put_part(0, solved, spread(collect(0)))
-    first_dir = exchange(0)
+    first_dir, _ = exchange(0)
     image = apply(first_dir, slice(0, high))
 
     set_total(image)
@@ -466,29 +476,38 @@
     solved = smooth(image)
     rows = collect(1)
     put_part(1, solved, spread(rows))
-    second_dir = exchange(1)[near]
-    first_dir, first_vector, image = first_dir[near], first_vector[near], image[near]
-    squares, mixed, image_squares = whole_sums(rows, 3)
-    source_norm = jnp.sqrt(squares + EPSILON)
-    shrink = 1.0 / source_norm
-    first_first = mixed * shrink * shrink
-    left_over = (
-        image_squares * shrink * shrink
-        - 2.0 * first_first * first_first
-        + first_first * first_first * (squares * shrink * shrink)
-    )
-    second_first = jnp.sqrt(jnp.maximum(left_over, 0.0) + EPSILON)
-    first = first_vector * shrink
-    first_dir = first_dir * shrink
-    second = (image * shrink - first_first * first) / second_first
-    second_dir = (second_dir * shrink - first_first * first_dir) / second_first
+
+    def first_column():
+        squares, mixed, image_squares = whole_sums(rows, 3)
+        source_norm = jnp.sqrt(squares + EPSILON)
+        shrink = 1.0 / source_norm
+        first_first = mixed * shrink * shrink
+        left_over = (
+            image_squares * shrink * shrink
+            - 2.0 * first_first * first_first
+            + first_first * first_first * (squares * shrink * shrink)
+        )
+        second_first = jnp.sqrt(jnp.maximum(left_over, 0.0) + EPSILON)
+        grow = 1.0 / second_first
+        first = first_vector_own * shrink
+        second = (image_own * shrink - first_first * first) * grow
+        radius_inverse = lax.rsqrt(first_first * first_first + second_first * second_first)
+        products = [(first, first), (second, second), (first, second)]
+        return (
+            source_norm, shrink, first_first, second_first, grow, first, second,
+            radius_inverse, first_first * radius_inverse, second_first * radius_inverse,
+            first_dir[near] * shrink, dots(products, 3),
+        )
+
+    second_dir, found = exchange(1, first_column)
+    (
+        source_norm, shrink, first_first, second_first, grow, first, second,
+        radius_inverse, cosine, sine, first_dir, known_dots,
+    ) = found
+    second_dir = (second_dir[near] * shrink - first_first * first_dir) * grow
     image = apply(second_dir, near)[middle]
     first_dir, second_dir = first_dir[middle], second_dir[middle]
-    first, second = first[middle], second[middle]
-    row_out[2] = dots(
-        [(first, image), (second, image), (image, image), (first, first), (second, second),
-         (first, second)]
-    )
+    row_out[2] = known_dots + dots([(first, image), (second, image), (image, image)])
     share(2)
     first_second, second_second, image_squares, ones, twos, cross = whole_sums(collect(2), 6)
     left_over = (
@@ -498,15 +517,18 @@
         + second_second * second_second * twos
         + 2.0 * first_second * second_second * cross
     )
-    third_second = jnp.sqrt(jnp.maximum(left_over, 0.0) + EPSILON)
+    third_square = jnp.maximum(left_over, 0.0) + EPSILON
     image = image - first_second * first - second_second * second
-    weight_one, weight_two, remainder_one, remainder_two, remainder_three = least_squares(
-        source_norm, first_first, second_first, first_second, second_second, third_second
-    )
+    upper_right = cosine * first_second + sine * second_second
+    lower_right = cosine * second_second - sine * first_second
+    weight_two = (
+        lower_right * (-sine * source_norm) / (lower_right * lower_right + third_square)
+    )
+    weight_one = (cosine * source_norm - upper_right * weight_two) * radius_inverse
+    remainder_one = source_norm - first_first * weight_one - first_second * weight_two
+    remainder_two = -second_first * weight_one - second_second * weight_two
     answer = weight_one * first_dir + weight_two * second_dir
-    remainder = (
-        remainder_one * first + remainder_two * second + (remainder_three / third_second) * image
-    )
+    remainder = remainder_one * first + remainder_two * second - weight_two * image
     both_out[0] = pltpu.roll(answer, wide - SIDE, 1)[:, :breadth]
     both_out[1] = pltpu.roll(remainder, wide - SIDE, 1)[:, :breadth]
 

time: 35.8 us -> 35.4 us (0.989)
  Pallas kernels: 32.9 us -> 32.5 us
where the time goes in v5:
time: 35.4 us; the launch traced here: 35.2 us
  Pallas kernels  32.5 us (92%)
  local copies, waits for them, and re-layouts  1.4 us (4%)
  between operations  1.29 us (4%)
    pallas_call x1, Pallas kernels, on_device(): pl.pallas_call(functools.partial(kernel, gx, gy, far), out_shape=jax.Shap...  32.5 us
    squeeze x1, local copies, waits for them, and re-layouts, on_device(): return (both[0], both[1])  1.4 us

profile of v5, /device:TPU:0, one launch (start us, length us, event | category | flops | bytes accessed | tf_op | source)
XLA Modules:
  0.0 35.2 jit_solution(17106109852200169235)
XLA Ops:
  1.3 32.5 %shard_map.95 = f32[2,32,256]{2,1,0:T(8,128)} custom-call(s32[1,1]{1,0:T(1,128)S(6)} %copy.10.counts_hbm, f32[32,256]{1,0:T(8,128)} %source.1, f32[32,256]{1,0:T(8,128)} %potential.1, f32[32,256]{1,0:T(8,128)} %along.1, f32[32,256]{1,0:T(8,128)} %across.1, f32[32,256]{1,0:T(8,128)} %recombination.1, f32[32,18432]{1,0:T(8,128)} %basis_hbm.1, ...), custom_call_target="tpu_custom_call" | custom-call | tf_op jit(solution)/shard_map/pallas_call | solution.py:562
  33.8 1.4 %slice_bitcast_fusion = (f32[32,256]{1,0:T(8,128)}, f32[32,256]{1,0:T(8,128)}) fusion(f32[2,32,256]{2,1,0:T(8,128)} %shard_map.95), kind=kLoop, calls=%fused_computation | loop fusion | bytes 131072 | tf_op jit(solution)/shard_map/squeeze | solution.py:592

commit v6 on v5

--- a/solution.py
+++ b/solution.py
@@ -14,11 +14,14 @@
 LANES = 128
 ROWS = 24
 SIDE = 64
+FOLD = 40
+FOLD_ROWS = 16
 NARROW = 8
 VMEM_GRANT = 63 * 1024 * 1024
 MESH = pl.DeviceIdType.MESH
 
 NEAR = [(i, j) for i in (-1, 0, 1) for j in (-1, 0, 1) if (i, j) != (0, 0)]
+CORNERS = [(i, j) for i in (-1, 1) for j in (-1, 1)]
 FAR = [(i, j) for i in (-2, 2) for j in (-1, 0, 1)]
 
 
@@ -50,7 +53,7 @@
     gx, gy, far,
     counts_hbm, source, potential, along, across, recombination, basis_hbm, inverse_hbm,
     both_out,
-    counts, basis, inverse, grown, raw, fields, pack_out, pack_in, part, total, flat, row_out,
+    counts, basis, inverse, grown, raw, fields, pack_out, pack_in, part, corners, total, flat, row_out,
     gathered, *rest,
 ):
     directions = (NEAR + far, NEAR)
@@ -76,9 +79,9 @@
     along_y = [wrapped(y, b, gy) if b else y for b in range(gy)] if few else []
 
     def to_others(act):
-        for a in range(gx):
+        for a in reversed(range(gx)):
             if few:
-                for b in range(gy):
+                for b in sorted(range(gy), key=lambda b: abs(2 * b - gy)):
                     if a or b:
                         act((along_x[a], along_y[b]))
             else:
@@ -159,14 +162,18 @@
     def part_copy(turn):
         def make(number, di, dj):
             rows, columns, _, _ = part_slices(turn, di, dj, height, breadth)
-            return copy(
-                part.at[turn, rows, columns], arrived[turn][number], 2 + turn, number, di, dj
-            )
+            src = part.at[turn, rows, columns]
+            if (di, dj) in CORNERS:
+                src = corners.at[turn, CORNERS.index((di, dj))]
+            return copy(src, arrived[turn][number], 2 + turn, number, di, dj)
 
         return make
 
-    def start_all(make, chosen):
+    def start_all(make, chosen, corner=None):
         for number, (di, dj) in enumerate(chosen):
+            if corner is not None and corner != ((di, dj) in CORNERS):
+                continue
+
             @pl.when(present(di, dj))
             def _(number=number, di=di, dj=dj):
                 make(number, di, dj).start()
@@ -362,8 +369,28 @@
             pltpu.roll(value, 1, 1),
         )
 
+    fold_lane = SIDE - OV - 4
+    fold_lanes = lax.broadcasted_iota(jnp.int32, (FOLD_ROWS, LANES), 1)
+    fold_place = fold_lanes // FOLD
+    in_fold = (fold_lanes >= fold_lane) & (fold_lanes < fold_lane + FOLD)
+
+    def folds(di):
+        away = [height + i * FOLD_ROWS for i in range(3)]
+        near_rows = [i * FOLD_ROWS for i in range(3)]
+        return (away, near_rows) if di == 1 else (near_rows, away)
+
     def exchange(turn, meanwhile=lambda: None):
-        start_all(part_copy(turn), directions[turn])
+        start_all(part_copy(turn), directions[turn], corner=False)
+        for number, (di, dj) in enumerate(CORNERS):
+            side = part[turn, :, wide - LANES:] if dj == 1 else part[turn, :, :LANES]
+            folded = jnp.zeros((FOLD_ROWS, LANES), jnp.float32)
+            for strip_number, row in enumerate(folds(di)[0]):
+                moved = pltpu.roll(
+                    side[row:row + FOLD_ROWS], (FOLD * strip_number - fold_lane) % LANES, 1
+                )
+                folded = jnp.where(fold_place == strip_number, moved, folded)
+            corners[turn, number] = folded
+        start_all(part_copy(turn), directions[turn], corner=True)
         set_total(part[turn])
         found = meanwhile()
         receive_all(part_copy(turn), directions[turn])
@@ -371,6 +398,13 @@
             _, _, rows, columns = part_slices(turn, di, dj, height, breadth)
             got = arrived[turn][number][...]
             first = columns.start // LANES
+            if (di, dj) in CORNERS:
+                for strip_number, row in enumerate(folds(di)[1]):
+                    moved = pltpu.roll(got, (fold_lane - FOLD * strip_number) % LANES, 1)
+                    moved = jnp.where(in_fold, moved, 0.0)
+                    at = pl.ds(row, FOLD_ROWS)
+                    total[first, at, :] = total[first, at, :] + moved
+                continue
             for t in range(columns.size // LANES):
                 total[first + t, rows, :] = (
                     total[first + t, rows, :] + got[:, t * LANES:(t + 1) * LANES]
@@ -509,6 +543,11 @@
     first_dir, second_dir = first_dir[middle], second_dir[middle]
     row_out[2] = known_dots + dots([(first, image), (second, image), (image, image)])
     share(2)
+    sent_all(source_copy, NEAR)
+    sent_all(field_copy, NEAR)
+    for turn in range(2):
+        sent_all(part_copy(turn), directions[turn])
+        row_bytes(turn, row_send).wait()
     first_second, second_second, image_squares, ones, twos, cross = whole_sums(collect(2), 6)
     left_over = (
         image_squares
@@ -531,13 +570,7 @@
     remainder = remainder_one * first + remainder_two * second - weight_two * image
     both_out[0] = pltpu.roll(answer, wide - SIDE, 1)[:, :breadth]
     both_out[1] = pltpu.roll(remainder, wide - SIDE, 1)[:, :breadth]
-
-    sent_all(source_copy, NEAR)
-    sent_all(field_copy, NEAR)
-    for turn in range(2):
-        sent_all(part_copy(turn), directions[turn])
-    for turn in range(3):
-        row_bytes(turn, row_send).wait()
+    row_bytes(2, row_send).wait()
 
 
 def on_device(
@@ -555,7 +588,10 @@
     for turn, chosen in enumerate((NEAR + far, NEAR)):
         for di, dj in chosen:
             rows, columns, _, _ = part_slices(turn, di, dj, height, breadth)
-            arrived.append(pltpu.VMEM((rows.size, columns.size), jnp.float32))
+            shape = (rows.size, columns.size)
+            if (di, dj) in CORNERS:
+                shape = (FOLD_ROWS, LANES)
+            arrived.append(pltpu.VMEM(shape, jnp.float32))
     vmem = pl.BlockSpec(memory_space=pltpu.VMEM)
     hbm = pl.BlockSpec(memory_space=pltpu.HBM)
     ways = len(NEAR + far)
@@ -574,6 +610,7 @@
             pltpu.VMEM((2, height, LANES), jnp.float32),
             pltpu.VMEM((2, high, LANES), jnp.float32),
             pltpu.VMEM((2, high, wide), jnp.float32),
+            pltpu.VMEM((2, len(CORNERS), FOLD_ROWS, LANES), jnp.float32),
             pltpu.VMEM((wide // LANES, high, LANES), jnp.float32),
             pltpu.VMEM((px // group, py * group), jnp.float32),
             pltpu.VMEM((3, 1, LANES), jnp.float32),

time: 35.4 us -> 34.9 us (0.986)
  Pallas kernels: 32.5 us -> 32 us
    pallas_call x1, Pallas kernels: 32.5 us -> 32 us  [on_device(): pl.pallas_call(functools.partial(kernel, gx, gy, far), out_shape=jax.Shap...]
where the time goes in v6:
time: 34.9 us; the launch traced here: 34.7 us
  Pallas kernels  32 us (92%)
  local copies, waits for them, and re-layouts  1.4 us (4%)
  between operations  1.29 us (4%)
    pallas_call x1, Pallas kernels, on_device(): pl.pallas_call(functools.partial(kernel, gx, gy, far), out_shape=jax.Shap...  32 us
    squeeze x1, local copies, waits for them, and re-layouts, on_device(): return (both[0], both[1])  1.4 us

profile of v6, /device:TPU:0, one launch (start us, length us, event | category | flops | bytes accessed | tf_op | source)
XLA Modules:
  0.0 34.7 jit_solution(4506900175603448777)
XLA Ops:
  1.3 32.0 %shard_map.95 = f32[2,32,256]{2,1,0:T(8,128)} custom-call(s32[1,1]{1,0:T(1,128)S(6)} %copy.10.counts_hbm, f32[32,256]{1,0:T(8,128)} %source.1, f32[32,256]{1,0:T(8,128)} %potential.1, f32[32,256]{1,0:T(8,128)} %along.1, f32[32,256]{1,0:T(8,128)} %across.1, f32[32,256]{1,0:T(8,128)} %recombination.1, f32[32,18432]{1,0:T(8,128)} %basis_hbm.1, ...), custom_call_target="tpu_custom_call" | custom-call | tf_op jit(solution)/shard_map/pallas_call | solution.py:598
  33.3 1.4 %slice_bitcast_fusion = (f32[32,256]{1,0:T(8,128)}, f32[32,256]{1,0:T(8,128)}) fusion(f32[2,32,256]{2,1,0:T(8,128)} %shard_map.95), kind=kLoop, calls=%fused_computation | loop fusion | bytes 131072 | tf_op jit(solution)/shard_map/squeeze | solution.py:629

commit v7 on v6

--- a/solution.py
+++ b/solution.py
@@ -21,6 +21,7 @@
 MESH = pl.DeviceIdType.MESH
 
 NEAR = [(i, j) for i in (-1, 0, 1) for j in (-1, 0, 1) if (i, j) != (0, 0)]
+UPRIGHT = [(-1, 0), (1, 0)]
 CORNERS = [(i, j) for i in (-1, 1) for j in (-1, 1)]
 FAR = [(i, j) for i in (-2, 2) for j in (-1, 0, 1)]
 
@@ -140,13 +141,21 @@
             grown.at[pl.ds(to, size), pl.ds(column_to, width)],
         )
 
-    def field_target(di, dj):
+    def field_target(di, dj, later=False):
         start, size, to = {
             0: (0, height, ROWS),
             1: (height - ROWS, ROWS, 0),
             -1: (0, ROWS, ROWS + height),
         }[di]
         if dj == 0:
+            if later:
+                size = ROWS - NARROW
+                if di == -1:
+                    start, to = start + NARROW, to + NARROW
+            else:
+                size = NARROW
+                if di == 1:
+                    start, to = start + ROWS - NARROW, to + ROWS - NARROW
             return (
                 fields.at[:, pl.ds(ROWS + start, size), :], fields.at[:, pl.ds(to, size), :]
             )
@@ -158,6 +167,9 @@
 
     def field_copy(number, di, dj):
         return copy(*field_target(di, dj), 1, number, di, dj)
+
+    def later_copy(number, di, dj):
+        return copy(*field_target(di, dj, True), 4, number, di, dj)
 
     def part_copy(turn):
         def make(number, di, dj):
@@ -219,6 +231,8 @@
                 targets += [
                     arrived[1][number], source_target(di, dj)[1], field_target(di, dj)[1]
                 ]
+            if (di, dj) in UPRIGHT:
+                targets.append(field_target(di, dj, True)[1])
             for target in targets:
                 target[...] = jnp.zeros(target.shape, jnp.float32)
 
@@ -247,6 +261,7 @@
     pack_out[0] = to_east
     pack_out[1] = to_west
     start_all(field_copy, NEAR)
+    start_all(later_copy, UPRIGHT)
     loads[5].wait()
 
     frame_row = lax.broadcasted_iota(jnp.int32, (high, wide), 0)
@@ -435,40 +450,49 @@
     row_out[0] = restrict()
     share(0)
 
-    receive_all(field_copy, NEAR)
-    patch = []
-    side_lane = lax.broadcasted_iota(jnp.int32, (high, LANES), 1)
-    for f in range(4):
-        base = jnp.concatenate([fields[f], jnp.zeros((high, LANES), jnp.float32)], axis=1)
-        base = pltpu.roll(base, SIDE, 1)
-        west = pltpu.roll(pack_in[0], (SIDE - (f + 1) * strip) % LANES, 1)
-        east = pltpu.roll(pack_in[1], (SIDE - f * strip) % LANES, 1)
-        left = jnp.where((side_lane >= SIDE - strip) & (side_lane < SIDE), west, base[:, :LANES])
-        right = jnp.where(
-            (side_lane >= SIDE) & (side_lane < SIDE + strip), east, base[:, wide - LANES:]
-        )
-        patch.append(jnp.concatenate([left, base[:, LANES:wide - LANES], right], axis=1))
-    level = jnp.exp(0.5 * patch[0])
-    level_inverse = jnp.exp(-0.5 * patch[0])
-    root_along, root_across = patch[1], patch[2]
-    faces = (
-        root_along * pltpu.roll(root_along, high - 1, 0),
-        root_along * pltpu.roll(root_along, 1, 0),
-        root_across * pltpu.roll(root_across, wide - 1, 1),
-        root_across * pltpu.roll(root_across, 1, 1),
-    )
-    outflow = jnp.zeros((high, wide), jnp.float32)
-    for face, beside in zip(faces, around(level_inverse)):
-        outflow = outflow + face * beside
-    diagonal = patch[3] + level * outflow
-    diagonal = jnp.where(diagonal > 0.0, diagonal, 1.0)
+    def build(rows):
+        count = rows.stop - rows.start
+        side_lane = lax.broadcasted_iota(jnp.int32, (count, LANES), 1)
+        patch = []
+        for f in range(4):
+            base = jnp.concatenate(
+                [fields[f, rows, :], jnp.zeros((count, LANES), jnp.float32)], axis=1
+            )
+            base = pltpu.roll(base, SIDE, 1)
+            west = pltpu.roll(pack_in[0, rows, :], (SIDE - (f + 1) * strip) % LANES, 1)
+            east = pltpu.roll(pack_in[1, rows, :], (SIDE - f * strip) % LANES, 1)
+            left = jnp.where(
+                (side_lane >= SIDE - strip) & (side_lane < SIDE), west, base[:, :LANES]
+            )
+            right = jnp.where(
+                (side_lane >= SIDE) & (side_lane < SIDE + strip), east, base[:, wide - LANES:]
+            )
+            patch.append(jnp.concatenate([left, base[:, LANES:wide - LANES], right], axis=1))
+        level = jnp.exp(0.5 * patch[0])
+        level_inverse = jnp.exp(-0.5 * patch[0])
+        root_along, root_across = patch[1], patch[2]
+        faces = (
+            root_along * pltpu.roll(root_along, count - 1, 0),
+            root_along * pltpu.roll(root_along, 1, 0),
+            root_across * pltpu.roll(root_across, wide - 1, 1),
+            root_across * pltpu.roll(root_across, 1, 1),
+        )
+        outflow = jnp.zeros((count, wide), jnp.float32)
+        for face, beside in zip(faces, around(level_inverse)):
+            outflow = outflow + face * beside
+        diagonal = patch[3] + level * outflow
+        diagonal = jnp.where(diagonal > 0.0, diagonal, 1.0)
+        return level, level_inverse, faces, diagonal
+
     near = slice(ROWS - NARROW, ROWS + height + NARROW)
     middle = slice(NARROW, NARROW + height)
     mine = slice(ROWS, ROWS + height)
-    step_size = OMEGA / diagonal[near]
-    step_faces = [face[near] * step_size for face in faces]
-    step_level = step_size * level[near]
-    own_level_inverse = level_inverse[mine]
+    receive_all(field_copy, NEAR)
+    level, level_inverse, faces, diagonal = build(near)
+    step_size = OMEGA / diagonal
+    step_faces = [face * step_size for face in faces]
+    step_level = step_size * level
+    own_level_inverse = level_inverse[middle]
 
     def smooth(vector):
         scaled = step_level * vector[near]
@@ -492,6 +516,8 @@
         part[turn, own_rows, :] = spreads[mine] + solved
 
     solved = smooth(first_vector)
+    receive_all(later_copy, UPRIGHT)
+    level, level_inverse, faces, diagonal = build(slice(0, high))
     loads[6].wait()
     put_part(0, solved, spread(collect(0)))
     first_dir, _ = exchange(0)
@@ -545,6 +571,7 @@
     share(2)
     sent_all(source_copy, NEAR)
     sent_all(field_copy, NEAR)
+    sent_all(later_copy, UPRIGHT)
     for turn in range(2):
         sent_all(part_copy(turn), directions[turn])
         row_bytes(turn, row_send).wait()
@@ -617,8 +644,8 @@
             pltpu.VMEM((3, devices, 1, LANES), jnp.float32),
             *arrived,
             pltpu.SemaphoreType.DMA((8,)),
-            pltpu.SemaphoreType.DMA((4, ways)),
-            pltpu.SemaphoreType.DMA((4, ways)),
+            pltpu.SemaphoreType.DMA((5, ways)),
+            pltpu.SemaphoreType.DMA((5, ways)),
             pltpu.SemaphoreType.DMA((3,)),
             pltpu.SemaphoreType.DMA((3,)),
         ],

time: 34.9 us -> 35 us (level)
  no operation moved by 1% of the time
where the time goes in v7:
time: 35 us; the launch traced here: 34.8 us
  Pallas kernels  32.1 us (92%)
  local copies, waits for them, and re-layouts  1.4 us (4%)
  between operations  1.29 us (4%)
    pallas_call x1, Pallas kernels, on_device(): pl.pallas_call(functools.partial(kernel, gx, gy, far), out_shape=jax.Shap...  32.1 us
    squeeze x1, local copies, waits for them, and re-layouts, on_device(): return (both[0], both[1])  1.4 us

profile of v7, /device:TPU:0, one launch (start us, length us, event | category | flops | bytes accessed | tf_op | source)
XLA Modules:
  0.0 34.8 jit_solution(14459844495131461100)
XLA Ops:
  1.3 32.1 %shard_map.95 = f32[2,32,256]{2,1,0:T(8,128)} custom-call(s32[1,1]{1,0:T(1,128)S(6)} %copy.10.counts_hbm, f32[32,256]{1,0:T(8,128)} %source.1, f32[32,256]{1,0:T(8,128)} %potential.1, f32[32,256]{1,0:T(8,128)} %along.1, f32[32,256]{1,0:T(8,128)} %across.1, f32[32,256]{1,0:T(8,128)} %recombination.1, f32[32,18432]{1,0:T(8,128)} %basis_hbm.1, ...), custom_call_target="tpu_custom_call" | custom-call | tf_op jit(solution)/shard_map/pallas_call | solution.py:625
  33.4 1.4 %slice_bitcast_fusion = (f32[32,256]{1,0:T(8,128)}, f32[32,256]{1,0:T(8,128)}) fusion(f32[2,32,256]{2,1,0:T(8,128)} %shard_map.95), kind=kLoop, calls=%fused_computation | loop fusion | bytes 131072 | tf_op jit(solution)/shard_map/squeeze | solution.py:656
